TPU v7x, 32 devices: a whole 2x2x4 slice. The times are simulated.
32 devices in a mesh: dp: 8 (over z, y), tensor: 4 (over x, core).
Axes of the slice: x: 2, y: 2, z: 4, core: 2. Of those that a mesh axis runs over, the one named last changes fastest.
Arguments:
- hidden_in: bfloat16 [8192, 2048], P(('dp', 'tensor')), may hold values from -6 to 6
- layer_input: bfloat16 [8192, 256], P(('dp', 'tensor')), may hold values from -6 to 6
- cached_len: int32 [16], replicated, may hold values from 3584 to 4096, as said below
- page_table: int32 [16, 32], replicated, may hold values from 0 to 511, as said below
- kv_pool: bfloat16 [512, 2, 2, 128, 256], P(('dp', 'tensor'))
- norm_in: float32 [2048], replicated, may hold values from 0.5 to 1.5
- w_query: bfloat16 [2048, 2048], P(None, 'tensor'), may hold values from -0.125 to 0.125
- w_keyval: bfloat16 [2048, 1024], replicated, may hold values from -0.125 to 0.125
- q_gain: float32 [256], replicated, may hold values from 0.1 to 0.4
- k_gain: float32 [256], replicated, may hold values from 0.5 to 1.5
- w_out: bfloat16 [2048, 2048], P('tensor'), may hold values from -0.125 to 0.125
- post_attn_gain: float32 [2048], replicated, may hold values from 0.5 to 1.5
- laurel_left: bfloat16 [2048, 64], replicated, may hold values from -0.125 to 0.125
- laurel_right: bfloat16 [64, 2048], replicated, may hold values from -0.75 to 0.75
- laurel_gain: float32 [2048], replicated, may hold values from 0.5 to 1.5
- pre_ffn_gain: float32 [2048], replicated, may hold values from 0.5 to 1.5
- w_gate: bfloat16 [2048, 8192], P(None, 'tensor'), may hold values from -0.125 to 0.125
- w_up: bfloat16 [2048, 8192], P(None, 'tensor'), may hold values from -0.125 to 0.125
- w_down: bfloat16 [8192, 2048], P('tensor'), may hold values from -0.0625 to 0.0625
- post_ffn_gain: float32 [2048], replicated, may hold values from 0.5 to 1.5
- ple_gate: bfloat16 [2048, 256], replicated, may hold values from -0.125 to 0.125
- ple_proj: bfloat16 [256, 2048], replicated, may hold values from -0.375 to 0.375
- ple_gain: float32 [2048], replicated, may hold values from 0.5 to 1.5
Outputs:
- layer_out: bfloat16 [8192, 2048], P(('dp', 'tensor'))
Inputs may be any that keep to these rules, and one draw needn't show every extreme that they name: `cached_len`: the last request of the first index of dp, and the last request of all, have 4096 cached tokens. `page_table`: page id q lives on the device with flat index q // 16 over dp+tensor (dp slowest), at row q % 16 of its shard. Only slots below ceil(cached_len / 128) are read; every slot names a page. Requests r with the same r // 8 name the same pages in their first 8 slots, and no other page is named twice. The slots that are read by the requests of one index of dp name at most 2 distinct pages of any one device, and some index of dp reaches 2.
All inputs are finite; a program needn't handle non-finite values.
Results may differ from a plain program's by a relative error of at most 0.015.
The roundings to bfloat16 on the way count: a program that leaves them out, or rounds other values in their place, can miss the bound.
Values may be sent and summed in bfloat16 or wider, within the bound.
A program may use at most 192 MiB of HBM per device.

v0:
```python
import functools
import math

import jax
import jax.numpy as jnp
from jax import lax
from jax.experimental import pallas as pl
from jax.experimental.pallas import tpu as pltpu
from jax.sharding import PartitionSpec as P

KVH = 2
PROMPT_PAGES = 8
REQ_DEV = 2


EPS = 1e-06
BIG = 1e30
KEY_BLOCK = 1024
SHORTEST = 3584
HALVES = 2
HALF_ROOT = 1.0 / math.sqrt(2.0)


def norm_rows(values, gain):
    return values * lax.rsqrt(jnp.mean(values * values, axis=-1, keepdims=True) + EPS) * gain


def rotate(values, position):
    half_dim = values.shape[-1] // 2
    freqs = jnp.exp(jnp.arange(half_dim, dtype=jnp.float32) * (-math.log(1000000.0) / half_dim))
    angle = position.astype(jnp.float32)[:, None] * freqs[None, :]
    cosine = jnp.cos(angle)[:, None, :]
    sine = jnp.sin(angle)[:, None, :]
    first = values[..., :half_dim]
    second = values[..., half_dim:]
    return jnp.concatenate(
        [first * cosine - second * sine, second * cosine + first * sine], axis=-1
    )


def attend_kernel(
    slots, place, lengths, core, q_ref, off_ref, kn_ref, vn_ref, mine, other, out_ref,
    keys, values, key_sem, value_sem
):
    request = pl.program_id(0)
    first_head = pl.program_id(1) == 0
    page_len = mine.shape[1]
    blocks = slots * page_len // KEY_BLOCK
    per_block = KEY_BLOCK // page_len

    def fetch(key_source, value_source):
        def one(index, carry):
            req = index // slots
            slot = index % slots
            block = slot // per_block
            rows = pl.ds(pl.multiple_of(slot * page_len, page_len), page_len)
            pltpu.make_async_copy(
                key_source.at[place[index]], keys.at[req, rows], key_sem.at[req, block]
            ).start()
            pltpu.make_async_copy(
                value_source.at[place[index]], values.at[req, rows], value_sem.at[req, block]
            ).start()
            return carry

        lax.fori_loop(0, REQ_DEV * slots, one, 0)

    @pl.when(jnp.logical_and(request == 0, first_head))
    def _():
        @pl.when(core[0] == 0)
        def _():
            fetch(mine, other)

        @pl.when(core[0] == 1)
        def _():
            fetch(other, mine)

    query = q_ref[0]
    fresh = kn_ref.shape[1]
    contract_last = (((1,), (1,)), ((), ()))
    score = lax.dot_general(query, kn_ref[0], contract_last, preferred_element_type=jnp.float32)
    visible = off_ref[...] >= lax.broadcasted_iota(jnp.int32, (query.shape[0], fresh), 1)
    score = jnp.where(visible, score, -BIG)
    top = jnp.max(score, axis=-1, keepdims=True)
    weight = jnp.exp(score - top)
    total = jnp.sum(weight, axis=-1, keepdims=True)
    mixed = jnp.dot(weight.astype(jnp.bfloat16), vn_ref[0], preferred_element_type=jnp.float32)
    for block in range(blocks):
        rows = pl.ds(block * KEY_BLOCK, KEY_BLOCK)

        @pl.when(first_head)
        def _():
            part = keys.at[request, rows]
            pltpu.make_async_copy(part, part, key_sem.at[request, block]).wait()
            part = values.at[request, rows]
            pltpu.make_async_copy(part, part, value_sem.at[request, block]).wait()

        score = lax.dot_general(
            query, keys[request, rows, :], contract_last, preferred_element_type=jnp.float32
        )
        if (block + 1) * KEY_BLOCK > SHORTEST:
            at = block * KEY_BLOCK + lax.broadcasted_iota(jnp.int32, score.shape, 1)
            score = jnp.where(at < lengths[request], score, -BIG)
        higher = jnp.maximum(top, jnp.max(score, axis=-1, keepdims=True))
        scale = jnp.exp(top - higher)
        weight = jnp.exp(score - higher)
        total = total * scale + jnp.sum(weight, axis=-1, keepdims=True)
        mixed = mixed * scale + jnp.dot(
            weight.astype(jnp.bfloat16), values[request, rows, :], preferred_element_type=jnp.float32
        )
        top = higher
    out_ref[0] = (mixed / total).astype(out_ref.dtype)


def attend(place, lengths, core, queries, offsets, fresh_keys, fresh_values, mine, other):
    requests, rows, width = queries.shape
    fresh, head_dim = fresh_keys.shape[1:]
    page_len = mine.shape[1]
    slots = place.shape[0] // requests
    heads = width // head_dim
    blocks = slots * page_len // KEY_BLOCK
    pairs = requests * heads * rows * (slots * page_len + fresh)
    return pl.pallas_call(
        functools.partial(attend_kernel, slots),
        out_shape=jax.ShapeDtypeStruct(queries.shape, jnp.bfloat16),
        grid_spec=pltpu.PrefetchScalarGridSpec(
            num_scalar_prefetch=3,
            grid=(requests, heads),
            in_specs=[
                pl.BlockSpec((1, rows, head_dim), lambda r, h, *_: (r, 0, h)),
                pl.BlockSpec((rows, 1), lambda r, h, *_: (0, 0)),
                pl.BlockSpec((1, fresh, head_dim), lambda r, h, *_: (r, 0, 0)),
                pl.BlockSpec((1, fresh, head_dim), lambda r, h, *_: (r, 0, 0)),
                pl.BlockSpec(memory_space=pl.ANY),
                pl.BlockSpec(memory_space=pl.ANY),
            ],
            out_specs=pl.BlockSpec((1, rows, head_dim), lambda r, h, *_: (r, 0, h)),
            scratch_shapes=[
                pltpu.VMEM((requests, slots * page_len, head_dim), jnp.bfloat16),
                pltpu.VMEM((requests, slots * page_len, head_dim), jnp.bfloat16),
                pltpu.SemaphoreType.DMA((requests, blocks)),
                pltpu.SemaphoreType.DMA((requests, blocks)),
            ],
        ),
        compiler_params=pltpu.CompilerParams(vmem_limit_bytes=28 * 1024 * 1024),
        cost_estimate=pl.CostEstimate(
            flops=4 * pairs * head_dim, bytes_accessed=2 * mine.size * 2, transcendentals=pairs
        ),
    )(place, lengths, core, queries, offsets, fresh_keys, fresh_values, mine, other)


def swap_cores(values, tp_count):
    return lax.ppermute(values, "tensor", [(t, t ^ 1) for t in range(tp_count)])


def shift_chips(values, tp_count, step):
    return lax.ppermute(values, "tensor", [(t, (t + 2 * step) % tp_count) for t in range(tp_count)])


def spread_rows(block, tp_count):
    pieces = [block, swap_cores(block, tp_count)]
    for step in range(1, tp_count // 2):
        came = shift_chips(block, tp_count, step)
        pieces += [came, swap_cores(came, tp_count)]
    return jnp.concatenate(pieces, axis=0)


def collect_rows(partial, tp_count):
    chips = tp_count // 2
    partial = partial.reshape(chips, 2, -1, partial.shape[-1])
    came = swap_cores(partial[:, 1].astype(jnp.bfloat16), tp_count)
    joined = partial[:, 0].astype(jnp.float32) + came.astype(jnp.float32)
    total = joined[0]
    for step in range(1, chips):
        came = shift_chips(joined[step].astype(jnp.bfloat16), tp_count, -step)
        total = total + came.astype(jnp.float32)
    return total


def geglu(block, w_gate, w_up):
    gate_part = jnp.dot(block, w_gate, preferred_element_type=jnp.float32)
    up_part = jnp.dot(block, w_up, preferred_element_type=jnp.float32)
    return (jax.nn.gelu(gate_part, approximate=True) * up_part).astype(jnp.bfloat16)


def per_device(
    hidden_in,
    layer_input,
    cached_len,
    page_table,
    kv_pool,
    norm_in,
    w_query,
    w_keyval,
    q_gain,
    k_gain,
    w_out,
    post_attn_gain,
    laurel_left,
    laurel_right,
    laurel_gain,
    pre_ffn_gain,
    w_gate,
    w_up,
    w_down,
    post_ffn_gain,
    ple_gate,
    ple_proj,
    ple_gain,
):
    dp_count = lax.axis_size("dp")
    tp_count = lax.axis_size("tensor")
    devices = dp_count * tp_count
    dp_at = lax.axis_index("dp")
    tp_at = lax.axis_index("tensor")
    chips = tp_count // 2
    chip_at = tp_at // 2
    core_at = tp_at % 2
    own_rows = hidden_in.shape[0]
    half_rows = own_rows // HALVES
    head_dim = q_gain.shape[0]
    local_heads = w_query.shape[1] // head_dim
    sharing = tp_count // KVH
    kv_head = tp_at // sharing
    slot_count = page_table.shape[1]
    page_len = kv_pool.shape[3]
    pool_dev = kv_pool.shape[0]
    needed = PROMPT_PAGES + REQ_DEV * (slot_count - PROMPT_PAGES)
    capacity = (needed + devices - 1) // devices
    page_count = (cached_len + page_len - 1) // page_len
    used_slots = jnp.arange(slot_count, dtype=jnp.int32)[None, :] < page_count[:, None]
    group_used = used_slots.reshape(dp_count, REQ_DEV * slot_count)
    group_table = page_table.reshape(dp_count, REQ_DEV * slot_count)
    own_flat = dp_at * tp_count + tp_at
    own_ids = own_flat * pool_dev + jnp.arange(pool_dev, dtype=jnp.int32)
    wanted = jnp.any(
        group_used[:, :, None] & (group_table[:, :, None] == own_ids[None, None, :]), axis=1
    )
    wanted_rank = jnp.cumsum(wanted.astype(jnp.int32), axis=1) - 1
    slot_ids = jnp.arange(capacity, dtype=jnp.int32)
    selector = (wanted[:, None, :] & (wanted_rank[:, None, :] == slot_ids[None, :, None])).astype(
        jnp.bfloat16
    )
    picked = jnp.einsum(
        "dcl,lkhpe->dhkcpe", selector, kv_pool, preferred_element_type=jnp.float32
    ).astype(jnp.bfloat16)
    outgoing = jnp.broadcast_to(
        picked[:, :, None],
        (dp_count, KVH, sharing // 2, 2, capacity, page_len, head_dim),
    ).reshape(devices, capacity, page_len, head_dim)
    arrived = lax.all_to_all(outgoing, ("dp", "tensor"), split_axis=0, concat_axis=0, tiled=True)
    mine = arrived.reshape(devices * capacity, page_len, head_dim)
    other = swap_cores(mine, tp_count)
    own_used = lax.dynamic_index_in_dim(group_used, dp_at, 0, keepdims=False)
    own_table = lax.dynamic_index_in_dim(group_table, dp_at, 0, keepdims=False)
    every_page = jnp.arange(devices * pool_dev, dtype=jnp.int32)
    present = jnp.any(own_used[None, :] & (own_table[None, :] == every_page[:, None]), axis=1)
    present_rank = (
        jnp.cumsum(present.reshape(devices, pool_dev).astype(jnp.int32), axis=1) - 1
    ).reshape(-1)
    place = jnp.where(own_used, own_table // pool_dev * capacity + present_rank[own_table], 0)
    own_lengths = lax.dynamic_slice_in_dim(cached_len, dp_at * REQ_DEV, REQ_DEV, 0)
    gathered = lax.all_gather(hidden_in, "tensor", axis=0, tiled=True)
    token_count = gathered.shape[0]
    new_count = token_count // REQ_DEV
    normed = norm_rows(gathered.astype(jnp.float32), norm_in).astype(jnp.bfloat16)
    offsets = jnp.arange(new_count, dtype=jnp.int32)
    position = (own_lengths[:, None] + offsets[None, :]).reshape(-1)
    queries = jnp.dot(normed, w_query, preferred_element_type=jnp.float32).reshape(
        token_count, local_heads, head_dim
    )
    queries = rotate(norm_rows(queries, q_gain), position).astype(jnp.bfloat16)
    key_weight = lax.dynamic_slice_in_dim(w_keyval, kv_head * head_dim, head_dim, 1)
    value_weight = lax.dynamic_slice_in_dim(w_keyval, (KVH + kv_head) * head_dim, head_dim, 1)
    fresh_keys = norm_rows(jnp.dot(normed, key_weight, preferred_element_type=jnp.float32), k_gain)
    fresh_keys = rotate(fresh_keys[:, None, :], position)[:, 0].astype(jnp.bfloat16)
    fresh_values = norm_rows(
        jnp.dot(normed, value_weight, preferred_element_type=jnp.float32), 1.0
    ).astype(jnp.bfloat16)
    fresh_keys = fresh_keys.reshape(REQ_DEV, new_count, head_dim)
    fresh_values = fresh_values.reshape(REQ_DEV, new_count, head_dim)
    by_half = (REQ_DEV, tp_count // REQ_DEV, HALVES, half_rows, local_heads * head_dim)
    queries = queries.reshape(by_half)
    offsets = offsets.reshape(by_half[1:4])

    own_x = hidden_in.astype(jnp.float32)
    own_normed = norm_rows(own_x, norm_in).astype(jnp.bfloat16)
    left_part = jnp.dot(own_normed, laurel_left, preferred_element_type=jnp.float32).astype(
        jnp.bfloat16
    )
    laurel_out = own_normed.astype(jnp.float32) + norm_rows(
        jnp.dot(left_part, laurel_right, preferred_element_type=jnp.float32), laurel_gain
    )
    beside = own_x + laurel_out

    owners = [
        (chip_at - step + chips) % chips * 2 + (core_at if same == 0 else 1 - core_at)
        for step in range(chips)
        for same in range(2)
    ]
    core_flag = core_at.reshape(1).astype(jnp.int32)
    projected = []
    for half in range(HALVES):
        attended = attend(
            place,
            own_lengths,
            core_flag,
            queries[:, :, half].reshape(REQ_DEV, new_count // HALVES, -1),
            offsets[:, half].reshape(-1, 1),
            fresh_keys,
            fresh_values,
            mine,
            other,
        ).reshape(tp_count, half_rows, -1)
        attended = jnp.concatenate(
            [lax.dynamic_index_in_dim(attended, owner, 0, keepdims=False) for owner in owners]
        )
        projected.append(
            collect_rows(jnp.dot(attended, w_out, preferred_element_type=jnp.float32), tp_count)
        )
    mixed_halves, entering = [], []
    for half in range(HALVES):
        rows = slice(half * half_rows, (half + 1) * half_rows)
        mixed_rows = (beside[rows] + norm_rows(projected[half], post_attn_gain)) * HALF_ROOT
        mixed_halves.append(mixed_rows)
        ffn_in = norm_rows(mixed_rows, pre_ffn_gain).astype(jnp.bfloat16)
        entering.append(spread_rows(ffn_in, tp_count))
    results = []
    for half in range(HALVES):
        rows = slice(half * half_rows, (half + 1) * half_rows)
        hidden = geglu(entering[half], w_gate, w_up)
        down = collect_rows(
            jnp.dot(hidden, w_down, preferred_element_type=jnp.float32).astype(jnp.bfloat16),
            tp_count,
        )
        settled = mixed_halves[half] + norm_rows(down, post_ffn_gain)
        settled_half = settled.astype(jnp.bfloat16)
        gated = jax.nn.gelu(
            jnp.dot(settled_half, ple_gate, preferred_element_type=jnp.float32), approximate=True
        )
        gated = (gated * layer_input[rows].astype(jnp.float32)).astype(jnp.bfloat16)
        results.append(
            (
                settled
                + norm_rows(
                    jnp.dot(gated, ple_proj, preferred_element_type=jnp.float32), ple_gain
                )
            ).astype(jnp.bfloat16)
        )
    return jnp.concatenate(results, axis=0)


def solution(mesh):
    placed = (
        P(("dp", "tensor"), None),
        P(("dp", "tensor"), None),
        P(),
        P(),
        P(("dp", "tensor"), None, None, None, None),
        P(),
        P(None, "tensor"),
        P(),
        P(),
        P(),
        P("tensor", None),
        P(),
        P(),
        P(),
        P(),
        P(),
        P(None, "tensor"),
        P(None, "tensor"),
        P("tensor", None),
        P(),
        P(),
        P(),
        P(),
    )
    return jax.shard_map(
        per_device, mesh=mesh, in_specs=placed, out_specs=P(("dp", "tensor"), None), check_vma=False
    )
```

profile of v0, /device:TPU:0, one launch (start us, length us, event | category | flops | bytes accessed | tf_op | source)
XLA Modules:
  0.0 348.6 jit_solution(11616892142737296177)
XLA Ops:
  9.0 4.7 %convert_bitcast_fusion = bf16[8,2,2,2,128,256]{5,0,4,1,2,3:T(8,128)(2,1)S(1)} fusion(bf16[16,2,2,128,256]{4,3,2,1,0:T(8,128)(2,1)} %param.27, s32[8,16]{1,0:T(8,128)S(1)} %broadcast_add_fusion.1, pred[8,16]{1,0:T(8,128)(4,1)S(1)} %and_reduce_fusion), kind=kOutput, calls=%fused_computation.29 | convolution fusion | flops 69206528 | bytes 8389248 | tf_op jit(solution)/shard_map/dcl,lkhpe->dhkcpe/dot_general | solution.py:243
  16.7 7.4 %all-to-all-start = ((bf16[32,2,128,256]{3,2,1,0:T(8,128)(2,1)}), bf16[32,2,128,256]{3,2,1,0:T(8,128)(2,1)}, u32[]{:S(2)}, u32[]{:S(2)}) async-start(bf16[32,2,128,256]{3,2,1,0:T(8,128)(2,1)} %bitcast.187), calls=%async_computation | async-start | bytes 8388608 | tf_op jit(solution)/shard_map/all_to_all | solution.py:250
  30.1 3.8 %multiply_reduce_fusion.1 = (f32[256]{0:T(256)S(1)}, f32[256,2048]{1,0:T(8,128)}) fusion(bf16[64,2048]{1,0:T(8,128)(2,1)} %param.36, bf16[2048,64]{0,1:T(8,128)(2,1)} %param.35, bf16[256,2048]{1,0:T(8,128)(2,1)S(1)} %copy-done.3, f32[2048]{0:T(1024)S(1)} %copy-done.16, f32[256]{0:T(256)S(1)} %add_rsqrt_fusion.5), kind=kOutput, calls=%fused_computation.58 | convolution fusion | flops 137379584 | bytes 3680256 | tf_op jit(solution)/shard_map/dot_general | solution.py:291
  33.9 56.3 %all-gather.2.cloned.1.call-done = bf16[1024,2048]{1,0:T(8,128)(2,1)} async-done(((bf16[256,2048]{1,0:T(8,128)(2,1)}), bf16[1024,2048]{1,0:T(8,128)(2,1)}) %all-gather.2.cloned.1.call-update) | async-done | bytes 4194320 | tf_op jit(solution)/shard_map/all_gather | solution.py:262
  93.3 24.9 %all-to-all-done = bf16[32,2,128,256]{3,2,1,0:T(8,128)(2,1)} async-done(((bf16[32,2,128,256]{3,2,1,0:T(8,128)(2,1)}), bf16[32,2,128,256]{3,2,1,0:T(8,128)(2,1)}, u32[]{:S(2)}, u32[]{:S(2)}) %all-to-all-start) | async-done | bytes 4194336 | tf_op jit(solution)/shard_map/all_to_all | solution.py:250
  118.2 4.0 %multiply_reduce_fusion.11 = (f32[1024]{0:T(1024)S(1)}, f32[1024,256]{0,1:T(8,128)S(1)}) fusion(bf16[2048,1024]{1,0:T(8,128)(2,1)} %param.30, s32[]{:T(128)S(6)} %select_n.88, bf16[1024,2048]{1,0:T(8,128)(2,1)} %all-gather.2.cloned.1.call-done, f32[2048]{0:T(1024)S(1)} %copy-done.16, f32[1024]{0:T(1024)S(1)} %add_rsqrt_fusion.3), kind=kOutput, calls=%fused_computation.102 | convolution fusion | flops 1082653696 | bytes 6307844 | tf_op jit(solution)/shard_map/dot_general | solution.py:274
  125.0 6.7 %multiply_reduce_fusion = (f32[1024,2]{0,1:T(2,128)S(1)}, f32[1024,512]{0,1:T(8,128)}) fusion(bf16[2048,512]{1,0:T(8,128)(2,1)} %param.29, bf16[1024,2048]{1,0:T(8,128)(2,1)} %all-gather.2.cloned.1.call-done, f32[2048]{0:T(1024)S(1)} %copy-done.16, f32[1024]{0:T(1024)S(1)} %add_rsqrt_fusion.3), kind=kOutput, calls=%fused_computation.57 | convolution fusion | flops 2156918784 | bytes 8409088 | tf_op jit(solution)/shard_map/dot_general | solution.py:268
  131.7 4.1 %copy.56 = f32[1024,2,256]{2,1,0:T(2,128)} copy(f32[1024,2,256]{0,2,1:T(8,128)} %bitcast.192) | data formatting | bytes 4194304 | tf_op jit(solution)/shard_map/reshape | solution.py:268
  145.0 4.0 %multiply_reduce_fusion.10 = (f32[1024]{0:T(1024)S(1)}, f32[1024,256]{1,0:T(8,128)S(1)}) fusion(bf16[2048,1024]{1,0:T(8,128)(2,1)} %param.30, s32[]{:T(128)S(6)} %select_n.89, bf16[1024,2048]{1,0:T(8,128)(2,1)} %all-gather.2.cloned.1.call-done, f32[2048]{0:T(1024)S(1)} %copy-done.16, f32[1024]{0:T(1024)S(1)} %add_rsqrt_fusion.3), kind=kOutput, calls=%fused_computation.98 | convolution fusion | flops 1082653696 | bytes 6307844 | tf_op jit(solution)/shard_map/dot_general | solution.py:277
  149.3 19.2 %shard_map.218 = bf16[2,256,512]{2,1,0:T(8,128)(2,1)S(1)} custom-call(s32[64]{0:T(128)S(1)} %add_select_fusion.place, s32[2]{0:T(128)S(1)} %dynamic_slice.44.lengths, s32[1]{0:T(128)} %bitcast.4.core, bf16[2,256,512]{2,1,0:T(8,128)(2,1)S(1)} %bitcast.186, s32[256,1]{1,0:T(8,128)S(1)} %copy.65.off_ref, bf16[2,512,256]{2,1,0:T(8,128)(2,1)S(1)} %bitcast.183, ...), custom_call_target="tpu_custom_call" | custom-call | flops 4831838208 | bytes 8388608 | tf_op jit(solution)/shard_map/pallas_call | solution.py:122
  168.5 19.2 %shard_map.217 = bf16[2,256,512]{2,1,0:T(8,128)(2,1)S(1)} custom-call(s32[64]{0:T(128)S(1)} %add_select_fusion.place, s32[2]{0:T(128)S(1)} %dynamic_slice.44.lengths, s32[1]{0:T(128)} %bitcast.4.core, bf16[2,256,512]{2,1,0:T(8,128)(2,1)S(1)} %bitcast.185, s32[256,1]{1,0:T(8,128)S(1)} %copy.60.off_ref, bf16[2,512,256]{2,1,0:T(8,128)(2,1)S(1)} %bitcast.184, ...), custom_call_target="tpu_custom_call" | custom-call | flops 4831838208 | bytes 8388608 | tf_op jit(solution)/shard_map/pallas_call | solution.py:122
  196.1 11.3 %collective-permute-done.9 = bf16[128,2048]{1,0:T(8,128)(2,1)S(1)} collective-permute-done((bf16[128,2048]{1,0:T(8,128)(2,1)S(1)}, bf16[128,2048]{1,0:T(8,128)(2,1)S(1)}, u32[]{:S(2)}, u32[]{:S(2)}) %collective-permute-start.9) | collective-permute-done | bytes 524320 | tf_op jit(solution)/shard_map/ppermute | solution.py:156
  207.7 10.4 %collective-permute-done.2 = bf16[128,2048]{1,0:T(8,128)(2,1)S(1)} collective-permute-done((bf16[128,2048]{1,0:T(8,128)(2,1)S(1)}, bf16[128,2048]{1,0:T(8,128)(2,1)S(1)}, u32[]{:S(2)}, u32[]{:S(2)}) %collective-permute-start.2) | collective-permute-done | bytes 524320 | tf_op jit(solution)/shard_map/ppermute | solution.py:156
  222.2 12.8 %collective-permute-done.11 = bf16[128,2048]{1,0:T(8,128)(2,1)S(1)} collective-permute-done((bf16[128,2048]{1,0:T(8,128)(2,1)S(1)}, bf16[128,2048]{1,0:T(8,128)(2,1)S(1)}, u32[]{:S(2)}, u32[]{:S(2)}) %collective-permute-start.11) | collective-permute-done | bytes 524320 | tf_op jit(solution)/shard_map/ppermute | solution.py:156
  235.5 9.4 %collective-permute-done.4 = bf16[128,2048]{1,0:T(8,128)(2,1)} collective-permute-done((bf16[128,2048]{1,0:T(8,128)(2,1)}, bf16[128,2048]{1,0:T(8,128)(2,1)}, u32[]{:S(2)}, u32[]{:S(2)}) %collective-permute-start.4) | collective-permute-done | bytes 524320 | tf_op jit(solution)/shard_map/ppermute | solution.py:156
  246.5 6.4 %fusion.89 = f32[512,2048]{1,0:T(8,128)} fusion(bf16[2048,2048]{1,0:T(8,128)(2,1)S(1)} %bitcast.202, bf16[128,2048]{1,0:T(8,128)(2,1)S(1)} %collective-permute-done.12, bf16[128,2048]{1,0:T(8,128)(2,1)S(1)} %collective-permute-done.11, bf16[128,2048]{1,0:T(8,128)(2,1)S(1)} %collective-permute-done.10, bf16[128,2048]{1,0:T(8,128)(2,1)S(1)} %get-tuple-element.28), kind=kOutput, calls=%fused_computation.146 | convolution fusion | flops 4303355904 | bytes 14680064 | tf_op jit(solution)/shard_map/dot_general | solution.py:180
  252.9 18.2 %convolution_convert_fusion = bf16[512,2048]{1,0:T(8,128)(2,1)} fusion(bf16[2048,2048]{1,0:T(8,128)(2,1)} %param.41, f32[512,2048]{1,0:T(8,128)} %fusion.89, bf16[2048,2048]{1,0:T(8,128)(2,1)} %param.40, bf16[128,2048]{1,0:T(8,128)(2,1)} %copy-done.24, bf16[128,2048]{1,0:T(8,128)(2,1)S(1)} %collective-permute-done.11, bf16[128,2048]{1,0:T(8,128)(2,1)} %copy-done.23, ...), kind=kOutput, calls=%fused_computation.33 | convolution fusion | flops 8609857536 | bytes 25165824 | tf_op jit(solution)/shard_map/dot_general | solution.py:332
  273.0 10.5 %fusion.91 = f32[512,2048]{1,0:T(8,128)} fusion(bf16[2048,2048]{1,0:T(8,128)(2,1)} %param.39, bf16[128,2048]{1,0:T(8,128)(2,1)} %collective-permute-done.5, bf16[128,2048]{1,0:T(8,128)(2,1)} %collective-permute-done.4, bf16[128,2048]{1,0:T(8,128)(2,1)} %collective-permute-done.3, bf16[128,2048]{1,0:T(8,128)(2,1)} %get-tuple-element.27), kind=kOutput, calls=%fused_computation.148 | convolution fusion | flops 4303355904 | bytes 14680064 | tf_op jit(solution)/shard_map/dot_general | solution.py:180
  283.5 18.7 %convolution_convert_fusion.1 = bf16[512,2048]{1,0:T(8,128)(2,1)} fusion(bf16[2048,2048]{1,0:T(8,128)(2,1)} %param.41, f32[512,2048]{1,0:T(8,128)} %fusion.91, bf16[2048,2048]{1,0:T(8,128)(2,1)} %param.40, bf16[128,2048]{1,0:T(8,128)(2,1)} %collective-permute-done.5, bf16[128,2048]{1,0:T(8,128)(2,1)} %collective-permute-done.4, ...), kind=kOutput, calls=%fused_computation.34 | convolution fusion | flops 8609857536 | bytes 25165824 | tf_op jit(solution)/shard_map/dot_general | solution.py:332
  309.2 11.4 %collective-permute-done.14 = bf16[128,2048]{1,0:T(8,128)(2,1)S(1)} collective-permute-done((bf16[128,2048]{1,0:T(8,128)(2,1)S(1)}, bf16[128,2048]{1,0:T(8,128)(2,1)S(1)}, u32[]{:S(2)}, u32[]{:S(2)}) %collective-permute-start.14) | collective-permute-done | bytes 524320 | tf_op jit(solution)/shard_map/ppermute | solution.py:156
  320.8 3.7 %multiply_reduce_fusion.2 = (f32[128]{0:T(128)S(1)}, f32[128,2048]{1,0:T(8,128)}) fusion(bf16[256,2048]{1,0:T(8,128)(2,1)} %param.44, bf16[2048,256]{1,0:T(8,128)(2,1)} %param.43, bf16[256,256]{1,0:T(8,128)(2,1)S(1)} %copy-done.14, f32[128,2048]{1,0:T(8,128)S(1)} %get-tuple-element.12, bf16[128,2048]{1,0:T(8,128)(2,1)S(1)} %collective-permute-done.14, ...), kind=kOutput, calls=%fused_computation.84 | convolution fusion | flops 271155072 | bytes 5841920 | tf_op jit(solution)/shard_map/dot_general | solution.py:345
  324.5 6.9 %collective-permute-done.7 = bf16[128,2048]{1,0:T(8,128)(2,1)S(1)} collective-permute-done((bf16[128,2048]{1,0:T(8,128)(2,1)}, bf16[128,2048]{1,0:T(8,128)(2,1)S(1)}, u32[]{:S(2)}, u32[]{:S(2)}) %collective-permute-start.7) | collective-permute-done | bytes 524320 | tf_op jit(solution)/shard_map/ppermute | solution.py:156
  333.0 3.7 %multiply_reduce_fusion.6 = (f32[128]{0:T(128)S(1)}, f32[128,2048]{1,0:T(8,128)}) fusion(bf16[256,2048]{1,0:T(8,128)(2,1)} %param.44, bf16[2048,256]{1,0:T(8,128)(2,1)} %param.43, bf16[256,256]{1,0:T(8,128)(2,1)S(1)} %copy-done.14, f32[128,2048]{1,0:T(8,128)S(1)} %get-tuple-element.6, bf16[128,2048]{1,0:T(8,128)(2,1)S(1)} %collective-permute-done.7, ...), kind=kOutput, calls=%fused_computation.91 | convolution fusion | flops 271155072 | bytes 5841920 | tf_op jit(solution)/shard_map/dot_general | solution.py:345
  336.7 3.7 %add_convert_fusion.1 = (bf16[128,2048]{1,0:T(8,128)(2,1)S(1)}, bf16[128,2048]{1,0:T(8,128)(2,1)S(1)}) fusion(f32[128,2048]{1,0:T(8,128)} %get-tuple-element.44, f32[2048]{0:T(1024)S(1)} %copy-done.20, f32[128]{0:T(128)S(1)} %add_rsqrt_fusion.9, f32[2048]{0:T(1024)S(1)} %copy-done.15, f32[128]{0:T(128)S(1)} %add_rsqrt_fusion.10, ...), kind=kLoop, calls=%fused_computation.90 | loop fusion | flops 5242880 | bytes 8407040 | tf_op jit(solution)/shard_map/convert_element_type | solution.py:347
  (170 shorter events, 52.8 us)
Async XLA Ops:
  6.5 181.3 %copy-start = (bf16[512,2048]{1,0:T(8,128)(2,1)S(1)}, bf16[512,2048]{1,0:T(8,128)(2,1)}, u32[]{:S(2)}) copy-start(bf16[512,2048]{1,0:T(8,128)(2,1)} %param.33) | copy-start | bytes 6291460
  16.7 101.6 %all-to-all-start = ((bf16[32,2,128,256]{3,2,1,0:T(8,128)(2,1)}), bf16[32,2,128,256]{3,2,1,0:T(8,128)(2,1)}, u32[]{:S(2)}, u32[]{:S(2)}) async-start(bf16[32,2,128,256]{3,2,1,0:T(8,128)(2,1)} %bitcast.187), calls=%async_computation | async-start | bytes 8388608 | tf_op jit(solution)/shard_map/all_to_all | solution.py:250
  24.1 66.1 %all-gather.2.cloned.1.call-start = ((), (), s32[]{:S(2)}) async-start(), calls=%async_computation.1 | async-start | bytes 5242880 | tf_op jit(solution)/shard_map/all_gather | solution.py:262
  118.2 31.0 %collective-permute-start = (bf16[64,128,256]{2,1,0:T(8,128)(2,1)}, bf16[64,128,256]{2,1,0:T(8,128)(2,1)}, u32[]{:S(2)}, u32[]{:S(2)}) collective-permute-start(bf16[64,128,256]{2,1,0:T(8,128)(2,1)} %bitcast.16.mine), channel_id=1, source_target_pairs={{0,1},{1,0},{2,3},{3,2},{4,5},{5,4},{6,7},{7,6},{8,9},{9,8},{10,11... | collective-permute-start | bytes 12582920 | tf_op jit(solution)/shard_map/ppermute | solution.py:152
  189.3 2.9 collective-permute-start.8
  191.3 2.7 collective-permute-start.1
  192.6 14.8 %collective-permute-start.9 = (bf16[128,2048]{1,0:T(8,128)(2,1)S(1)}, bf16[128,2048]{1,0:T(8,128)(2,1)S(1)}, u32[]{:S(2)}, u32[]{:S(2)}) collective-permute-start(bf16[128,2048]{1,0:T(8,128)(2,1)S(1)} %fusion.66), channel_id=1, source_target_pairs={{0,2},{1,3},{2,0},{3,1},{4,6},{5,7},{6,4},{7,5},{8,10},{9,11},{10,... | collective-permute-start | bytes 1572872 | tf_op jit(solution)/shard_map/ppermute | solution.py:156
  194.4 23.7 %collective-permute-start.2 = (bf16[128,2048]{1,0:T(8,128)(2,1)S(1)}, bf16[128,2048]{1,0:T(8,128)(2,1)S(1)}, u32[]{:S(2)}, u32[]{:S(2)}) collective-permute-start(bf16[128,2048]{1,0:T(8,128)(2,1)S(1)} %fusion.64), channel_id=1, source_target_pairs={{0,2},{1,3},{2,0},{3,1},{4,6},{5,7},{6,4},{7,5},{8,10},{9,11},{10,... | collective-permute-start | bytes 1572872 | tf_op jit(solution)/shard_map/ppermute | solution.py:156
  195.5 22.9 %copy-start.18 = (f32[2048]{0:T(1024)S(1)}, f32[2048]{0:T(1024)}, u32[]{:S(2)}) copy-start(f32[2048]{0:T(1024)} %param.34) | copy-start | bytes 24580
  195.5 51.0 %slice-start = ((s8[8388608]{0:T(1024)(128)(4,1)}), s8[4194304]{0:T(1024)(128)(4,1)S(1)}, s32[]{:S(2)}) async-start(s8[8388608]{0:T(1024)(128)(4,1)} %bitcast.201), calls=%async_computation.2 | async-start | bytes 8388608
  218.4 28.1 %slice-start.1 = ((s8[8388608]{0:T(1024)(128)(4,1)}), s8[4194304]{0:T(1024)(128)(4,1)S(1)}, s32[]{:S(2)}) async-start(s8[8388608]{0:T(1024)(128)(4,1)} %bitcast.201), calls=%async_computation.3 | async-start | bytes 8388608
  219.2 101.6 %copy-start.2 = (f32[128,2048]{1,0:T(8,128)}, f32[128,2048]{1,0:T(8,128)S(1)}, u32[]{:S(2)}) copy-start(f32[128,2048]{1,0:T(8,128)S(1)} %get-tuple-element.12) | copy-start | bytes 3145732
  220.2 14.8 %collective-permute-start.11 = (bf16[128,2048]{1,0:T(8,128)(2,1)S(1)}, bf16[128,2048]{1,0:T(8,128)(2,1)S(1)}, u32[]{:S(2)}, u32[]{:S(2)}) collective-permute-start(bf16[128,2048]{1,0:T(8,128)(2,1)S(1)} %get-tuple-element.28), channel_id=1, source_target_pairs={{0,2},{1,3},{2,0},{3,1},{4,6},{5,7},{6,4},{7,5},{8,10},{9,11},{10,... | collective-permute-start | bytes 1572872 | tf_op jit(solution)/shard_map/ppermute | solution.py:156
  221.2 23.7 %collective-permute-start.4 = (bf16[128,2048]{1,0:T(8,128)(2,1)}, bf16[128,2048]{1,0:T(8,128)(2,1)}, u32[]{:S(2)}, u32[]{:S(2)}) collective-permute-start(bf16[128,2048]{1,0:T(8,128)(2,1)} %get-tuple-element.27), channel_id=1, source_target_pairs={{0,2},{1,3},{2,0},{3,1},{4,6},{5,7},{6,4},{7,5},{8,10},{9,11},{10,... | collective-permute-start | bytes 1572872 | tf_op jit(solution)/shard_map/ppermute | solution.py:156
  222.2 22.7 %collective-permute-start.10 = (bf16[128,2048]{1,0:T(8,128)(2,1)S(1)}, bf16[128,2048]{1,0:T(8,128)(2,1)S(1)}, u32[]{:S(2)}, u32[]{:S(2)}) collective-permute-start(bf16[128,2048]{1,0:T(8,128)(2,1)S(1)} %get-tuple-element.28), channel_id=1, source_target_pairs={{0,1},{1,0},{2,3},{3,2},{4,5},{5,4},{6,7},{7,6},{8,9},{9,8},{10,11... | collective-permute-start | bytes 1572872 | tf_op jit(solution)/shard_map/ppermute | solution.py:152
  235.0 9.9 %collective-permute-start.12 = (bf16[128,2048]{1,0:T(8,128)(2,1)S(1)}, bf16[128,2048]{1,0:T(8,128)(2,1)S(1)}, u32[]{:S(2)}, u32[]{:S(2)}) collective-permute-start(bf16[128,2048]{1,0:T(8,128)(2,1)S(1)} %collective-permute-done.11), channel_id=1, source_target_pairs={{0,1},{1,0},{2,3},{3,2},{4,5},{5,4},{6,7},{7,6},{8,9},{9,8},{10,11... | collective-permute-start | bytes 1572872 | tf_op jit(solution)/shard_map/ppermute | solution.py:152
  235.0 38.0 %collective-permute-start.3 = (bf16[128,2048]{1,0:T(8,128)(2,1)}, bf16[128,2048]{1,0:T(8,128)(2,1)}, u32[]{:S(2)}, u32[]{:S(2)}) collective-permute-start(bf16[128,2048]{1,0:T(8,128)(2,1)} %get-tuple-element.27), channel_id=1, source_target_pairs={{0,1},{1,0},{2,3},{3,2},{4,5},{5,4},{6,7},{7,6},{8,9},{9,8},{10,11... | collective-permute-start | bytes 1572872 | tf_op jit(solution)/shard_map/ppermute | solution.py:152
  244.9 28.1 %collective-permute-start.5 = (bf16[128,2048]{1,0:T(8,128)(2,1)}, bf16[128,2048]{1,0:T(8,128)(2,1)}, u32[]{:S(2)}, u32[]{:S(2)}) collective-permute-start(bf16[128,2048]{1,0:T(8,128)(2,1)} %collective-permute-done.4), channel_id=1, source_target_pairs={{0,1},{1,0},{2,3},{3,2},{4,5},{5,4},{6,7},{7,6},{8,9},{9,8},{10,11... | collective-permute-start | bytes 1572872 | tf_op jit(solution)/shard_map/ppermute | solution.py:152
  272.4 31.3 %collective-permute-start.13 = (bf16[2,128,2048]{2,1,0:T(8,128)(2,1)S(1)}, bf16[2,128,2048]{2,1,0:T(8,128)(2,1)}, u32[]{:S(2)}, u32[]{:S(2)}) collective-permute-start(bf16[2,128,2048]{2,1,0:T(8,128)(2,1)S(1)} %slice_bitcast_fusion.1), channel_id=1, source_target_pairs={{0,1},{1,0},{2,3},{3,2},{4,5},{5,4},{6,7},{7,6},{8,9},{9,8},{10,11... | collective-permute-start | bytes 3145736 | tf_op jit(solution)/shard_map/ppermute | solution.py:152
  303.7 3.2 collective-permute-start.6
  305.7 15.1 %copy-start.14 = (bf16[256,256]{1,0:T(8,128)(2,1)S(1)}, bf16[256,256]{1,0:T(8,128)(2,1)}, u32[]{:S(2)}) copy-start(bf16[256,256]{1,0:T(8,128)(2,1)} %param.24) | copy-start | bytes 393220
  305.7 15.1 %copy-start.15 = (f32[2048]{0:T(1024)S(1)}, f32[2048]{0:T(1024)}, u32[]{:S(2)}) copy-start(f32[2048]{0:T(1024)} %param.42) | copy-start | bytes 24580
  305.8 14.8 %collective-permute-start.14 = (bf16[128,2048]{1,0:T(8,128)(2,1)S(1)}, bf16[128,2048]{1,0:T(8,128)(2,1)S(1)}, u32[]{:S(2)}, u32[]{:S(2)}) collective-permute-start(bf16[128,2048]{1,0:T(8,128)(2,1)S(1)} %fusion.67), channel_id=1, source_target_pairs={{0,2},{1,3},{2,0},{3,1},{4,6},{5,7},{6,4},{7,5},{8,10},{9,11},{10,... | collective-permute-start | bytes 1572872 | tf_op jit(solution)/shard_map/ppermute | solution.py:156
  308.1 23.2 %collective-permute-start.7 = (bf16[128,2048]{1,0:T(8,128)(2,1)}, bf16[128,2048]{1,0:T(8,128)(2,1)S(1)}, u32[]{:S(2)}, u32[]{:S(2)}) collective-permute-start(bf16[128,2048]{1,0:T(8,128)(2,1)} %fusion.65), channel_id=1, source_target_pairs={{0,2},{1,3},{2,0},{3,1},{4,6},{5,7},{6,4},{7,5},{8,10},{9,11},{10,... | collective-permute-start | bytes 1572872 | tf_op jit(solution)/shard_map/ppermute | solution.py:156
  (21 other events, 128.3 us)
Sparse Core Ops, SparseCore 0:
  26.5 63.6 all-gather.1
where the time goes:
time: 353 us; the launch traced here: 349 us
  waiting for transfers between devices  145 us (41%)
  matrix products  86.8 us (25%)
  Pallas kernels  38.5 us (11%)
  other arithmetic  29.1 us (8%)
  local copies, waits for them, and re-layouts  19.1 us (5%)
  starting transfers between devices  15.8 us (4%)
  between operations  14.4 us (4%)
    ppermute x6, waiting for transfers between devices, shift_chips(): lax.ppermute(values, 'tensor', [(t, (t + 2 * step) % tp_count) for t in r...  62.2 us
    all_gather x1, waiting for transfers between devices, per_device(): gathered = lax.all_gather(hidden_in, 'tensor', axis=0, tiled=True)  56.3 us
    pallas_call x2, Pallas kernels, attend(): pl.pallas_call(functools.partial(attend_kernel, slots), out_shape=jax.Sha...  38.5 us
    dot_general x2, matrix products, per_device(): jnp.dot(hidden, w_down, preferred_element_type=jnp.float32)  36.9 us
    all_to_all x1, waiting for transfers between devices, per_device(): lax.all_to_all(outgoing, ('dp', 'tensor'), split_axis=0, concat_axis=0, t...  24.9 us
    dot_general x2, matrix products, geglu(): gate_part = jnp.dot(block, w_gate, preferred_element_type=jnp.float32)  16.8 us
    all_to_all x1, starting transfers between devices, per_device(): lax.all_to_all(outgoing, ('dp', 'tensor'), split_axis=0, concat_axis=0, t...  7.43 us
    dot_general x2, matrix products, per_device(): jnp.dot(gated, ple_proj, preferred_element_type=jnp.float32)  7.35 us
  transfers between devices with their start and end apart: 17, of which 10 were waited for; matrix products, arithmetic and copies ran while one was open for 31% of the time, Pallas kernels for 0%

commit v1 on v0

--- a/solution.py
+++ b/solution.py
@@ -74,10 +74,32 @@
         def _():
             fetch(other, mine)
 
+    @pl.when(first_head)
+    def _():
+        for block in range(blocks):
+            rows = pl.ds(block * KEY_BLOCK, KEY_BLOCK)
+            part = keys.at[request, rows]
+            pltpu.make_async_copy(part, part, key_sem.at[request, block]).wait()
+            part = values.at[request, rows]
+            pltpu.make_async_copy(part, part, value_sem.at[request, block]).wait()
+
     query = q_ref[0]
     fresh = kn_ref.shape[1]
-    contract_last = (((1,), (1,)), ((), ()))
-    score = lax.dot_general(query, kn_ref[0], contract_last, preferred_element_type=jnp.float32)
+
+    def match(block_keys):
+        return lax.dot_general(
+            query, block_keys, (((1,), (1,)), ((), ())), preferred_element_type=jnp.float32
+        )
+
+    def cached(block):
+        score = match(keys[request, pl.ds(block * KEY_BLOCK, KEY_BLOCK), :])
+        if (block + 1) * KEY_BLOCK > SHORTEST:
+            at = block * KEY_BLOCK + lax.broadcasted_iota(jnp.int32, score.shape, 1)
+            score = jnp.where(at < lengths[request], score, -BIG)
+        return score
+
+    score = match(kn_ref[0])
+    ahead = cached(0)
     visible = off_ref[...] >= lax.broadcasted_iota(jnp.int32, (query.shape[0], fresh), 1)
     score = jnp.where(visible, score, -BIG)
     top = jnp.max(score, axis=-1, keepdims=True)
@@ -85,27 +107,17 @@
     total = jnp.sum(weight, axis=-1, keepdims=True)
     mixed = jnp.dot(weight.astype(jnp.bfloat16), vn_ref[0], preferred_element_type=jnp.float32)
     for block in range(blocks):
-        rows = pl.ds(block * KEY_BLOCK, KEY_BLOCK)
-
-        @pl.when(first_head)
-        def _():
-            part = keys.at[request, rows]
-            pltpu.make_async_copy(part, part, key_sem.at[request, block]).wait()
-            part = values.at[request, rows]
-            pltpu.make_async_copy(part, part, value_sem.at[request, block]).wait()
-
-        score = lax.dot_general(
-            query, keys[request, rows, :], contract_last, preferred_element_type=jnp.float32
-        )
-        if (block + 1) * KEY_BLOCK > SHORTEST:
-            at = block * KEY_BLOCK + lax.broadcasted_iota(jnp.int32, score.shape, 1)
-            score = jnp.where(at < lengths[request], score, -BIG)
+        score = ahead
+        if block + 1 < blocks:
+            ahead = cached(block + 1)
         higher = jnp.maximum(top, jnp.max(score, axis=-1, keepdims=True))
         scale = jnp.exp(top - higher)
         weight = jnp.exp(score - higher)
         total = total * scale + jnp.sum(weight, axis=-1, keepdims=True)
         mixed = mixed * scale + jnp.dot(
-            weight.astype(jnp.bfloat16), values[request, rows, :], preferred_element_type=jnp.float32
+            weight.astype(jnp.bfloat16),
+            values[request, pl.ds(block * KEY_BLOCK, KEY_BLOCK), :],
+            preferred_element_type=jnp.float32,
         )
         top = higher
     out_ref[0] = (mixed / total).astype(out_ref.dtype)
@@ -161,25 +173,65 @@
     for step in range(1, tp_count // 2):
         came = shift_chips(block, tp_count, step)
         pieces += [came, swap_cores(came, tp_count)]
-    return jnp.concatenate(pieces, axis=0)
-
-
-def collect_rows(partial, tp_count):
-    chips = tp_count // 2
-    partial = partial.reshape(chips, 2, -1, partial.shape[-1])
+    return pieces
+
+
+def join_cores(partial, tp_count):
     came = swap_cores(partial[:, 1].astype(jnp.bfloat16), tp_count)
-    joined = partial[:, 0].astype(jnp.float32) + came.astype(jnp.float32)
-    total = joined[0]
-    for step in range(1, chips):
-        came = shift_chips(joined[step].astype(jnp.bfloat16), tp_count, -step)
+    return partial[:, 0].astype(jnp.float32) + came.astype(jnp.float32)
+
+
+def join_chips(joined, total, tp_count):
+    for step in range(1, joined.shape[0] + 1):
+        came = shift_chips(joined[step - 1].astype(jnp.bfloat16), tp_count, -step)
         total = total + came.astype(jnp.float32)
     return total
 
 
-def geglu(block, w_gate, w_up):
-    gate_part = jnp.dot(block, w_gate, preferred_element_type=jnp.float32)
-    up_part = jnp.dot(block, w_up, preferred_element_type=jnp.float32)
-    return (jax.nn.gelu(gate_part, approximate=True) * up_part).astype(jnp.bfloat16)
+def ffn_kernel(x_ref, gate_ref, up_ref, down_ref, out_ref, total):
+    step = pl.program_id(0)
+    block = x_ref[...]
+    gate_part = jnp.dot(block, gate_ref[...], preferred_element_type=jnp.float32)
+    up_part = jnp.dot(block, up_ref[...], preferred_element_type=jnp.float32)
+    hidden = (jax.nn.gelu(gate_part, approximate=True) * up_part).astype(jnp.bfloat16)
+    part = jnp.dot(hidden, down_ref[...], preferred_element_type=jnp.float32)
+
+    @pl.when(step == 0)
+    def _():
+        total[...] = part
+
+    @pl.when(step > 0)
+    def _():
+        total[...] += part
+
+    @pl.when(step == pl.num_programs(0) - 1)
+    def _():
+        out_ref[...] = total[...].astype(out_ref.dtype)
+
+
+def feed_forward(block, w_gate, w_up, w_down):
+    rows, width = block.shape
+    units = w_gate.shape[1]
+    tile = min(512, units)
+    return pl.pallas_call(
+        ffn_kernel,
+        out_shape=jax.ShapeDtypeStruct(block.shape, jnp.bfloat16),
+        grid=(units // tile,),
+        in_specs=[
+            pl.BlockSpec((rows, width), lambda i: (0, 0)),
+            pl.BlockSpec((width, tile), lambda i: (0, i)),
+            pl.BlockSpec((width, tile), lambda i: (0, i)),
+            pl.BlockSpec((tile, width), lambda i: (i, 0)),
+        ],
+        out_specs=pl.BlockSpec((rows, width), lambda i: (0, 0)),
+        scratch_shapes=[pltpu.VMEM((rows, width), jnp.float32)],
+        compiler_params=pltpu.CompilerParams(vmem_limit_bytes=40 * 1024 * 1024),
+        cost_estimate=pl.CostEstimate(
+            flops=6 * rows * width * units,
+            bytes_accessed=6 * width * units,
+            transcendentals=rows * units,
+        ),
+    )(block, w_gate, w_up, w_down)
 
 
 def per_device(
@@ -248,8 +300,6 @@
         (dp_count, KVH, sharing // 2, 2, capacity, page_len, head_dim),
     ).reshape(devices, capacity, page_len, head_dim)
     arrived = lax.all_to_all(outgoing, ("dp", "tensor"), split_axis=0, concat_axis=0, tiled=True)
-    mine = arrived.reshape(devices * capacity, page_len, head_dim)
-    other = swap_cores(mine, tp_count)
     own_used = lax.dynamic_index_in_dim(group_used, dp_at, 0, keepdims=False)
     own_table = lax.dynamic_index_in_dim(group_table, dp_at, 0, keepdims=False)
     every_page = jnp.arange(devices * pool_dev, dtype=jnp.int32)
@@ -259,7 +309,15 @@
     ).reshape(-1)
     place = jnp.where(own_used, own_table // pool_dev * capacity + present_rank[own_table], 0)
     own_lengths = lax.dynamic_slice_in_dim(cached_len, dp_at * REQ_DEV, REQ_DEV, 0)
-    gathered = lax.all_gather(hidden_in, "tensor", axis=0, tiled=True)
+    near = jnp.stack(spread_rows(hidden_in, tp_count))
+    gathered = jnp.concatenate(
+        [
+            lax.dynamic_index_in_dim(
+                near, (chip_at - t // 2 + chips) % chips * 2 + (core_at + t) % 2, 0, keepdims=False
+            )
+            for t in range(tp_count)
+        ]
+    )
     token_count = gathered.shape[0]
     new_count = token_count // REQ_DEV
     normed = norm_rows(gathered.astype(jnp.float32), norm_in).astype(jnp.bfloat16)
@@ -279,6 +337,11 @@
     fresh_keys = fresh_keys.reshape(REQ_DEV, new_count, head_dim)
     fresh_values = fresh_values.reshape(REQ_DEV, new_count, head_dim)
     by_half = (REQ_DEV, tp_count // REQ_DEV, HALVES, half_rows, local_heads * head_dim)
+    arrived, queries, fresh_keys, fresh_values = lax.optimization_barrier(
+        (arrived, queries, fresh_keys, fresh_values)
+    )
+    mine = arrived.reshape(devices * capacity, page_len, head_dim)
+    other = swap_cores(mine, tp_count)
     queries = queries.reshape(by_half)
     offsets = offsets.reshape(by_half[1:4])
 
@@ -298,13 +361,17 @@
         for same in range(2)
     ]
     core_flag = core_at.reshape(1).astype(jnp.int32)
-    projected = []
+    width = hidden_in.shape[1]
+    joined = []
     for half in range(HALVES):
+        half_queries = queries[:, :, half].reshape(REQ_DEV, new_count // HALVES, -1)
+        if half:
+            half_queries, joined[-1] = lax.optimization_barrier((half_queries, joined[-1]))
         attended = attend(
             place,
             own_lengths,
             core_flag,
-            queries[:, :, half].reshape(REQ_DEV, new_count // HALVES, -1),
+            half_queries,
             offsets[:, half].reshape(-1, 1),
             fresh_keys,
             fresh_values,
@@ -314,24 +381,31 @@
         attended = jnp.concatenate(
             [lax.dynamic_index_in_dim(attended, owner, 0, keepdims=False) for owner in owners]
         )
-        projected.append(
-            collect_rows(jnp.dot(attended, w_out, preferred_element_type=jnp.float32), tp_count)
-        )
+        partial = jnp.dot(attended, w_out, preferred_element_type=jnp.float32)
+        joined.append(join_cores(partial.reshape(chips, 2, half_rows, width), tp_count))
     mixed_halves, entering = [], []
     for half in range(HALVES):
         rows = slice(half * half_rows, (half + 1) * half_rows)
-        mixed_rows = (beside[rows] + norm_rows(projected[half], post_attn_gain)) * HALF_ROOT
+        projected = join_chips(joined[half][1:], joined[half][0], tp_count)
+        mixed_rows = (beside[rows] + norm_rows(projected, post_attn_gain)) * HALF_ROOT
         mixed_halves.append(mixed_rows)
         ffn_in = norm_rows(mixed_rows, pre_ffn_gain).astype(jnp.bfloat16)
         entering.append(spread_rows(ffn_in, tp_count))
+    near_down, far_down = [], []
+    last = None
+    for pick, kept in ((slice(0, 2), near_down), (slice(2, None), far_down)):
+        for half in range(HALVES):
+            block = jnp.concatenate(entering[half][pick])
+            if last is not None:
+                block, last[-1] = lax.optimization_barrier((block, last[-1]))
+            kept.append(feed_forward(block, w_gate, w_up, w_down))
+            last = kept
     results = []
     for half in range(HALVES):
         rows = slice(half * half_rows, (half + 1) * half_rows)
-        hidden = geglu(entering[half], w_gate, w_up)
-        down = collect_rows(
-            jnp.dot(hidden, w_down, preferred_element_type=jnp.float32).astype(jnp.bfloat16),
-            tp_count,
-        )
+        near_sum = join_cores(near_down[half].reshape(1, 2, half_rows, width), tp_count)[0]
+        far_sum = join_cores(far_down[half].reshape(chips - 1, 2, half_rows, width), tp_count)
+        down = join_chips(far_sum, near_sum, tp_count)
         settled = mixed_halves[half] + norm_rows(down, post_ffn_gain)
         settled_half = settled.astype(jnp.bfloat16)
         gated = jax.nn.gelu(

time: 353 us -> 299 us (0.85)
  matrix products: 86.8 us -> 28.9 us
  waiting for transfers between devices: 145 us -> 112 us
  Pallas kernels: 38.5 us -> 67.9 us
  between operations: 14.4 us -> 1.01 us
  other arithmetic: 29.1 us -> 42.1 us
  local copies, waits for them, and re-layouts: 19.1 us -> 23.4 us
    all_gather x1 -> x0, waiting for transfers between devices: 56.3 us -> none  [per_device(): gathered = lax.all_gather(hidden_in, 'tensor', axis=0, tiled=True)]
    dot_general x6 -> x2, matrix products: 56.3 us -> 2.59 us  [per_device(): partial = jnp.dot(attended, w_out, preferred_element_type=jnp.float32)]
    ppermute x6 -> x7, waiting for transfers between devices: 62.2 us -> 111 us  [shift_chips(): lax.ppermute(values, 'tensor', [(t, (t + 2 * step) % tp_count) for t in r...]
    pallas_call x0 -> x4, Pallas kernels: none -> 45.3 us  [feed_forward(): pl.pallas_call(ffn_kernel, out_shape=jax.ShapeDtypeStruct(block.shape, jn...]
    all_to_all x1, waiting for transfers between devices: 24.9 us -> 0.01 us  [per_device(): lax.all_to_all(outgoing, ('dp', 'tensor'), split_axis=0, concat_axis=0, t...]
    pallas_call x2, Pallas kernels: 38.5 us -> 22.6 us  [attend(): pl.pallas_call(functools.partial(attend_kernel, slots), out_shape=jax.Sha...]
    convert_element_type x0 -> x3, other arithmetic: none -> 8.22 us  [the longest x1 7.17 us: per_device(): norm_rows(gathered.astype(jnp.float32), norm_in).astype(jnp.bfloat16)]
    ppermute x6 -> x7, starting transfers between devices: 6.26 us -> 8.33 us  [shift_chips(): lax.ppermute(values, 'tensor', [(t, (t + 2 * step) % tp_count) for t in r...]
  transfers between devices with their start and end apart: 17 -> 21, of which waited for: 10 -> 8; matrix products, arithmetic and copies ran while one was open for 31% -> 21% of each run, Pallas kernels for 0% -> 15%
where the time goes in v1:
time: 299 us; the launch traced here: 294 us
  waiting for transfers between devices  112 us (37%)
  Pallas kernels  67.9 us (23%)
  other arithmetic  42.1 us (14%)
  matrix products  28.9 us (10%)
  local copies, waits for them, and re-layouts  23.4 us (8%)
  starting transfers between devices  19.1 us (6%)
    ppermute x7, waiting for transfers between devices, shift_chips(): lax.ppermute(values, 'tensor', [(t, (t + 2 * step) % tp_count) for t in r...  111 us
    pallas_call x4, Pallas kernels, feed_forward(): pl.pallas_call(ffn_kernel, out_shape=jax.ShapeDtypeStruct(block.shape, jn...  45.3 us
    pallas_call x2, Pallas kernels, attend(): pl.pallas_call(functools.partial(attend_kernel, slots), out_shape=jax.Sha...  22.6 us
    ppermute x7, starting transfers between devices, shift_chips(): lax.ppermute(values, 'tensor', [(t, (t + 2 * step) % tp_count) for t in r...  8.33 us
    dot_general x2, matrix products, per_device(): jnp.dot(gated, ple_proj, preferred_element_type=jnp.float32)  7.8 us
    all_to_all x1, starting transfers between devices, per_device(): lax.all_to_all(outgoing, ('dp', 'tensor'), split_axis=0, concat_axis=0, t...  7.6 us
    convert_element_type x1, other arithmetic, per_device(): norm_rows(gathered.astype(jnp.float32), norm_in).astype(jnp.bfloat16)  7.17 us
  transfers between devices with their start and end apart: 21, of which 8 were waited for; matrix products, arithmetic and copies ran while one was open for 21% of the time, Pallas kernels for 15%

profile of v1, /device:TPU:0, one launch (start us, length us, event | category | flops | bytes accessed | tf_op | source)
XLA Modules:
  0.0 294.4 jit_solution(9879215828243086175)
XLA Ops:
  2.5 4.7 %convert_bitcast_fusion = bf16[8,2,2,2,128,256]{5,0,4,1,2,3:T(8,128)(2,1)S(1)} fusion(bf16[16,2,2,128,256]{4,3,2,1,0:T(8,128)(2,1)} %param.27, s32[8,16]{1,0:T(8,128)S(1)} %broadcast_add_fusion.1, pred[8,16]{1,0:T(8,128)(4,1)S(1)} %and_reduce_fusion), kind=kOutput, calls=%fused_computation.11 | convolution fusion | flops 69206528 | bytes 8389248 | tf_op jit(solution)/shard_map/dcl,lkhpe->dhkcpe/dot_general | solution.py:295
  10.2 7.6 %all-to-all-start = ((bf16[32,2,128,256]{3,2,1,0:T(8,128)(2,1)}), bf16[32,2,128,256]{3,2,1,0:T(8,128)(2,1)}, u32[]{:S(2)}, u32[]{:S(2)}) async-start(bf16[32,2,128,256]{3,2,1,0:T(8,128)(2,1)} %bitcast.228), calls=%async_computation | async-start | bytes 8388608 | tf_op jit(solution)/shard_map/all_to_all | solution.py:302
  19.7 62.7 %collective-permute-done.1 = bf16[256,2048]{1,0:T(8,128)(2,1)} collective-permute-done((bf16[256,2048]{1,0:T(8,128)(2,1)S(1)}, bf16[256,2048]{1,0:T(8,128)(2,1)}, u32[]{:S(2)}, u32[]{:S(2)}) %collective-permute-start.1) | collective-permute-done | bytes 1048608 | tf_op jit(solution)/shard_map/ppermute | solution.py:168
  82.6 3.0 %multiply_cosine_fusion.1 = (f32[1024,128]{1,0:T(8,128)}, f32[1024,128]{1,0:T(8,128)}) fusion(f32[128]{0:T(128)S(1)} %multiply_exponential_fusion, f32[1024]{0:T(1024)S(1)} %bitcast.235), kind=kLoop, calls=%fused_computation.86 | loop fusion | flops 131072 | bytes 1053184 | tf_op jit(solution)/shard_map/cos | solution.py:32
  89.4 7.2 %fusion.2 = bf16[1024,2048]{1,0:T(8,128)(2,1)S(1)} fusion(f32[2048]{0:T(1024)S(1)} %copy-done.22, f32[1024]{0:T(1024)S(1)} %add_rsqrt_fusion.3, bf16[256,2048]{1,0:T(8,128)(2,1)S(1)} %get-tuple-element.34, bf16[256,2048]{1,0:T(8,128)(2,1)S(1)} %get-tuple-element.35, bf16[256,2048]{1,0:T(8,128)(2,1)S(1)} %get-tuple-element.36, ...), kind=kLoop, calls=%fused_computation.5 | loop fusion | flops 23068672 | bytes 8400896 | tf_op jit(solution)/shard_map/convert_element_type | solution.py:323
  96.6 3.7 %multiply_reduce_fusion = (f32[1024,2]{0,1:T(2,128)S(1)}, f32[1024,512]{0,1:T(8,128)}) fusion(bf16[1024,2048]{1,0:T(8,128)(2,1)S(1)} %fusion.2, bf16[2048,512]{1,0:T(8,128)(2,1)S(1)} %copy-done.30), kind=kOutput, calls=%fused_computation.25 | convolution fusion | flops 2148530176 | bytes 8396800 | tf_op jit(solution)/shard_map/dot_general | solution.py:326
  100.3 4.2 %copy.50 = f32[1024,2,256]{2,1,0:T(2,128)} copy(f32[1024,2,256]{0,2,1:T(8,128)} %bitcast.234) | data formatting | bytes 4194304 | tf_op jit(solution)/shard_map/reshape | solution.py:326
  104.7 3.8 %multiply_reduce_fusion.11 = (f32[1024]{0:T(1024)S(1)}, f32[1024,256]{0,1:T(8,128)S(1)}) fusion(bf16[1024,2048]{1,0:T(8,128)(2,1)} %copy-done.16, bf16[2048,1024]{1,0:T(8,128)(2,1)} %param.30, s32[]{:T(128)S(6)} %select_n.131), kind=kOutput, calls=%fused_computation.73 | convolution fusion | flops 1074265088 | bytes 6295556 | tf_op jit(solution)/shard_map/dot_general | solution.py:332
  129.8 11.1 %shard_map.217 = bf16[2,256,512]{2,1,0:T(8,128)(2,1)S(1)} custom-call(s32[64]{0:T(128)S(1)} %add_select_fusion.place, s32[2]{0:T(128)S(1)} %dynamic_slice.59.lengths, s32[1]{0:T(128)} %bitcast.22.core, bf16[2,256,512]{2,1,0:T(8,128)(2,1)S(1)} %bitcast.227, s32[256,1]{1,0:T(8,128)S(1)} %copy.52.off_ref, bf16[2,512,256]{2,1,0:T(8,128)(2,1)S(1)} %bitcast.222, ...), custom_call_target="tpu_custom_call" | custom-call | flops 4831838208 | bytes 8388608 | tf_op jit(solution)/shard_map/pallas_call | solution.py:134
  146.5 3.6 %fusion.12 = f32[2,128,2048]{2,1,0:T(8,128)} fusion(bf16[2,128,2048]{2,1,0:T(8,128)(2,1)} %collective-permute-done.4, f32[2,2,128,2048]{3,2,1,0:T(8,128)} %bitcast.233), kind=kLoop, calls=%fused_computation.23 | loop fusion | flops 1048576 | bytes 5242880 | tf_op jit(solution)/shard_map/add | solution.py:181
  150.1 11.5 %shard_map.218 = bf16[2,256,512]{2,1,0:T(8,128)(2,1)S(1)} custom-call(s32[64]{0:T(128)S(1)} %add_select_fusion.place, s32[2]{0:T(128)S(1)} %dynamic_slice.59.lengths, s32[1]{0:T(128)} %bitcast.22.core, bf16[2,256,512]{2,1,0:T(8,128)(2,1)S(1)} %bitcast.226, s32[256,1]{1,0:T(8,128)S(1)} %copy.55.off_ref, bf16[2,512,256]{2,1,0:T(8,128)(2,1)S(1)} %bitcast.223, ...), custom_call_target="tpu_custom_call" | custom-call | flops 4831838208 | bytes 8388608 | tf_op jit(solution)/shard_map/pallas_call | solution.py:134
  165.5 3.8 %multiply_reduce_fusion.1 = (f32[256]{0:T(256)S(1)}, f32[256,2048]{1,0:T(8,128)}) fusion(bf16[64,2048]{1,0:T(8,128)(2,1)S(1)} %copy-done.20, bf16[2048,64]{0,1:T(8,128)(2,1)} %param.35, bf16[256,2048]{1,0:T(8,128)(2,1)S(1)} %copy-done.9, f32[2048]{0:T(1024)S(1)} %copy-done.22, f32[256]{0:T(256)S(1)} %add_rsqrt_fusion.5), kind=kOutput, calls=%fused_computation.26 | convolution fusion | flops 137379584 | bytes 3680256 | tf_op jit(solution)/shard_map/dot_general | solution.py:354
  175.4 10.0 %collective-permute-done.5 = bf16[128,2048]{1,0:T(8,128)(2,1)S(1)} collective-permute-done((bf16[128,2048]{1,0:T(8,128)(2,1)S(1)}, bf16[128,2048]{1,0:T(8,128)(2,1)S(1)}, u32[]{:S(2)}, u32[]{:S(2)}) %collective-permute-start.5) | collective-permute-done | bytes 524320 | tf_op jit(solution)/shard_map/ppermute | solution.py:168
  185.7 10.2 %collective-permute-done.7 = bf16[128,2048]{1,0:T(8,128)(2,1)S(1)} collective-permute-done((bf16[128,2048]{1,0:T(8,128)(2,1)S(1)}, bf16[128,2048]{1,0:T(8,128)(2,1)S(1)}, u32[]{:S(2)}, u32[]{:S(2)}) %collective-permute-start.7) | collective-permute-done | bytes 524320 | tf_op jit(solution)/shard_map/ppermute | solution.py:168
  199.4 11.3 %shard_map.219 = bf16[256,2048]{1,0:T(8,128)(2,1)S(1)} custom-call(bf16[256,2048]{1,0:T(8,128)(2,1)S(1)} %pad_maximum_fusion.4.x_ref, bf16[2048,2048]{1,0:T(8,128)(2,1)S(1)} %bitcast.207, bf16[2048,2048]{1,0:T(8,128)(2,1)} %up_ref.7, bf16[2048,2048]{1,0:T(8,128)(2,1)} %down_ref.7), custom_call_target="tpu_custom_call" | custom-call | flops 6442450944 | bytes 25165824 | tf_op jit(solution)/shard_map/pallas_call | solution.py:216
  211.4 11.3 %collective-permute-done.11 = bf16[128,2048]{1,0:T(8,128)(2,1)S(1)} collective-permute-done((bf16[128,2048]{1,0:T(8,128)(2,1)S(1)}, bf16[128,2048]{1,0:T(8,128)(2,1)S(1)}, u32[]{:S(2)}, u32[]{:S(2)}) %collective-permute-start.11) | collective-permute-done | bytes 524320 | tf_op jit(solution)/shard_map/ppermute | solution.py:168
  223.3 11.3 %shard_map.220 = bf16[256,2048]{1,0:T(8,128)(2,1)S(1)} custom-call(bf16[256,2048]{1,0:T(8,128)(2,1)S(1)} %pad_maximum_fusion.3.x_ref, bf16[2048,2048]{1,0:T(8,128)(2,1)S(1)} %bitcast.207, bf16[2048,2048]{1,0:T(8,128)(2,1)} %up_ref.7, bf16[2048,2048]{1,0:T(8,128)(2,1)} %down_ref.7), custom_call_target="tpu_custom_call" | custom-call | flops 6442450944 | bytes 25165824 | tf_op jit(solution)/shard_map/pallas_call | solution.py:216
  234.7 11.3 %shard_map.221 = bf16[256,2048]{1,0:T(8,128)(2,1)S(1)} custom-call(bf16[256,2048]{1,0:T(8,128)(2,1)S(1)} %pad_maximum_fusion.6.x_ref, bf16[2048,2048]{1,0:T(8,128)(2,1)S(1)} %bitcast.207, bf16[2048,2048]{1,0:T(8,128)(2,1)} %up_ref.7, bf16[2048,2048]{1,0:T(8,128)(2,1)} %down_ref.7), custom_call_target="tpu_custom_call" | custom-call | flops 6442450944 | bytes 25165824 | tf_op jit(solution)/shard_map/pallas_call | solution.py:216
  246.2 11.4 %shard_map.222 = bf16[256,2048]{1,0:T(8,128)(2,1)S(1)} custom-call(bf16[256,2048]{1,0:T(8,128)(2,1)S(1)} %pad_maximum_fusion.5.x_ref, bf16[2048,2048]{1,0:T(8,128)(2,1)S(1)} %bitcast.207, bf16[2048,2048]{1,0:T(8,128)(2,1)} %up_ref.7, bf16[2048,2048]{1,0:T(8,128)(2,1)} %down_ref.7), custom_call_target="tpu_custom_call" | custom-call | flops 6442450944 | bytes 25165824 | tf_op jit(solution)/shard_map/pallas_call | solution.py:216
  262.3 11.0 %collective-permute-done.16 = bf16[128,2048]{1,0:T(8,128)(2,1)S(1)} collective-permute-done((bf16[128,2048]{1,0:T(8,128)(2,1)S(1)}, bf16[128,2048]{1,0:T(8,128)(2,1)S(1)}, u32[]{:S(2)}, u32[]{:S(2)}) %collective-permute-start.16) | collective-permute-done | bytes 524320 | tf_op jit(solution)/shard_map/ppermute | solution.py:168
  274.1 4.1 %multiply_reduce_fusion.4 = (f32[128]{0:T(128)S(1)}, f32[128,2048]{1,0:T(8,128)}) fusion(bf16[256,2048]{1,0:T(8,128)(2,1)} %param.44, bf16[2048,256]{1,0:T(8,128)(2,1)} %param.43, bf16[256,256]{1,0:T(8,128)(2,1)S(1)} %copy-done.21, f32[128,2048]{1,0:T(8,128)} %copy-done.5, bf16[128,2048]{1,0:T(8,128)(2,1)} %copy-done.15, ...), kind=kOutput, calls=%fused_computation.59 | convolution fusion | flops 271941504 | bytes 5841920 | tf_op jit(solution)/shard_map/dot_general | solution.py:419
  278.2 5.5 %collective-permute-done.19 = bf16[128,2048]{1,0:T(8,128)(2,1)} collective-permute-done((bf16[128,2048]{1,0:T(8,128)(2,1)}, bf16[128,2048]{1,0:T(8,128)(2,1)}, u32[]{:S(2)}, u32[]{:S(2)}) %collective-permute-start.19) | collective-permute-done | bytes 524320 | tf_op jit(solution)/shard_map/ppermute | solution.py:168
  285.2 3.7 %multiply_reduce_fusion.2 = (f32[128]{0:T(128)S(1)}, f32[128,2048]{1,0:T(8,128)}) fusion(bf16[256,2048]{1,0:T(8,128)(2,1)} %param.44, bf16[2048,256]{1,0:T(8,128)(2,1)} %param.43, bf16[256,256]{1,0:T(8,128)(2,1)S(1)} %copy-done.21, f32[128,2048]{1,0:T(8,128)S(1)} %copy-done.7, bf16[128,2048]{1,0:T(8,128)(2,1)} %collective-permute-done.19, ...), kind=kOutput, calls=%fused_computation.55 | convolution fusion | flops 271941504 | bytes 5841920 | tf_op jit(solution)/shard_map/dot_general | solution.py:419
  289.0 4.1 %add_convert_fusion.1 = (bf16[128,2048]{1,0:T(8,128)(2,1)S(1)}, bf16[128,2048]{1,0:T(8,128)(2,1)S(1)}) fusion(f32[128,2048]{1,0:T(8,128)} %get-tuple-element.72, f32[2048]{0:T(1024)S(1)} %copy-done.27, f32[128]{0:T(128)S(1)} %add_rsqrt_fusion.8, f32[2048]{0:T(1024)S(1)} %copy-done.23, f32[128]{0:T(128)S(1)} %add_rsqrt_fusion.9, ...), kind=kLoop, calls=%fused_computation.58 | loop fusion | flops 6815744 | bytes 8407040 | tf_op jit(solution)/shard_map/convert_element_type | solution.py:421
  (196 shorter events, 61.3 us)
Async XLA Ops:
  0.0 141.0 %copy-start = (bf16[512,2048]{1,0:T(8,128)(2,1)S(1)}, bf16[512,2048]{1,0:T(8,128)(2,1)}, u32[]{:S(2)}) copy-start(bf16[512,2048]{1,0:T(8,128)(2,1)} %param.33) | copy-start | bytes 6291460
  10.2 72.2 %copy-start.31 = (s32[16]{0:T(128)S(1)}, s32[16]{0:T(128)}, u32[]{:S(2)}) copy-start(s32[16]{0:T(128)} %param.25) | copy-start | bytes 196
  10.2 111.9 %all-to-all-start = ((bf16[32,2,128,256]{3,2,1,0:T(8,128)(2,1)}), bf16[32,2,128,256]{3,2,1,0:T(8,128)(2,1)}, u32[]{:S(2)}, u32[]{:S(2)}) async-start(bf16[32,2,128,256]{3,2,1,0:T(8,128)(2,1)} %bitcast.228), calls=%async_computation | async-start | bytes 8388608 | tf_op jit(solution)/shard_map/all_to_all | solution.py:302
  17.8 64.6 %collective-permute-start.1 = (bf16[256,2048]{1,0:T(8,128)(2,1)S(1)}, bf16[256,2048]{1,0:T(8,128)(2,1)}, u32[]{:S(2)}, u32[]{:S(2)}) collective-permute-start(bf16[256,2048]{1,0:T(8,128)(2,1)S(1)} %copy-done.8), channel_id=1, source_target_pairs={{0,2},{1,3},{2,0},{3,1},{4,6},{5,7},{6,4},{7,5},{8,10},{9,11},{10,... | collective-permute-start | bytes 3145736 | tf_op jit(solution)/shard_map/ppermute | solution.py:168
  19.7 65.9 %collective-permute-start = (bf16[256,2048]{1,0:T(8,128)(2,1)S(1)}, bf16[256,2048]{1,0:T(8,128)(2,1)}, u32[]{:S(2)}, u32[]{:S(2)}) collective-permute-start(bf16[256,2048]{1,0:T(8,128)(2,1)S(1)} %copy-done.8), channel_id=1, source_target_pairs={{0,1},{1,0},{2,3},{3,2},{4,5},{5,4},{6,7},{7,6},{8,9},{9,8},{10,11... | collective-permute-start | bytes 3145736 | tf_op jit(solution)/shard_map/ppermute | solution.py:164
  82.4 3.2 %collective-permute-start.2 = (bf16[256,2048]{1,0:T(8,128)(2,1)}, bf16[256,2048]{1,0:T(8,128)(2,1)}, u32[]{:S(2)}, u32[]{:S(2)}) collective-permute-start(bf16[256,2048]{1,0:T(8,128)(2,1)} %collective-permute-done.1), channel_id=1, source_target_pairs={{0,1},{1,0},{2,3},{3,2},{4,5},{5,4},{6,7},{7,6},{8,9},{9,8},{10,11... | collective-permute-start | bytes 3145736 | tf_op jit(solution)/shard_map/ppermute | solution.py:164
  122.1 7.7 %collective-permute-start.3 = (bf16[64,128,256]{2,1,0:T(8,128)(2,1)}, bf16[64,128,256]{2,1,0:T(8,128)(2,1)}, u32[]{:S(2)}, u32[]{:S(2)}) collective-permute-start(bf16[64,128,256]{2,1,0:T(8,128)(2,1)} %bitcast.25.mine), channel_id=1, source_target_pairs={{0,1},{1,0},{2,3},{3,2},{4,5},{5,4},{6,7},{7,6},{8,9},{9,8},{10,11... | collective-permute-start | bytes 12582920 | tf_op jit(solution)/shard_map/ppermute | solution.py:164
  143.5 3.0 %collective-permute-start.4 = (bf16[2,128,2048]{2,1,0:T(8,128)(2,1)}, bf16[2,128,2048]{2,1,0:T(8,128)(2,1)}, u32[]{:S(2)}, u32[]{:S(2)}) collective-permute-start(bf16[2,128,2048]{2,1,0:T(8,128)(2,1)} %fusion.14), channel_id=1, source_target_pairs={{0,1},{1,0},{2,3},{3,2},{4,5},{5,4},{6,7},{7,6},{8,9},{9,8},{10,11... | collective-permute-start | bytes 3145736 | tf_op jit(solution)/shard_map/ppermute | solution.py:164
  165.1 7.1 %collective-permute-start.6 = (bf16[2,128,2048]{2,1,0:T(8,128)(2,1)S(1)}, bf16[2,128,2048]{2,1,0:T(8,128)(2,1)S(1)}, u32[]{:S(2)}, u32[]{:S(2)}) collective-permute-start(bf16[2,128,2048]{2,1,0:T(8,128)(2,1)S(1)} %fusion.15), channel_id=1, source_target_pairs={{0,1},{1,0},{2,3},{3,2},{4,5},{5,4},{6,7},{7,6},{8,9},{9,8},{10,11... | collective-permute-start | bytes 3145736 | tf_op jit(solution)/shard_map/ppermute | solution.py:164
  170.6 14.8 %collective-permute-start.5 = (bf16[128,2048]{1,0:T(8,128)(2,1)S(1)}, bf16[128,2048]{1,0:T(8,128)(2,1)S(1)}, u32[]{:S(2)}, u32[]{:S(2)}) collective-permute-start(bf16[128,2048]{1,0:T(8,128)(2,1)S(1)} %fusion.41), channel_id=1, source_target_pairs={{0,2},{1,3},{2,0},{3,1},{4,6},{5,7},{6,4},{7,5},{8,10},{9,11},{10,... | collective-permute-start | bytes 1572872 | tf_op jit(solution)/shard_map/ppermute | solution.py:168
  174.2 21.7 %collective-permute-start.7 = (bf16[128,2048]{1,0:T(8,128)(2,1)S(1)}, bf16[128,2048]{1,0:T(8,128)(2,1)S(1)}, u32[]{:S(2)}, u32[]{:S(2)}) collective-permute-start(bf16[128,2048]{1,0:T(8,128)(2,1)S(1)} %fusion.42), channel_id=1, source_target_pairs={{0,2},{1,3},{2,0},{3,1},{4,6},{5,7},{6,4},{7,5},{8,10},{9,11},{10,... | collective-permute-start | bytes 1572872 | tf_op jit(solution)/shard_map/ppermute | solution.py:168
  197.1 2.2 collective-permute-start.9
  197.2 25.6 %collective-permute-start.13 = (bf16[128,2048]{1,0:T(8,128)(2,1)S(1)}, bf16[128,2048]{1,0:T(8,128)(2,1)S(1)}, u32[]{:S(2)}, u32[]{:S(2)}) collective-permute-start(bf16[128,2048]{1,0:T(8,128)(2,1)S(1)} %get-tuple-element.55), channel_id=1, source_target_pairs={{0,2},{1,3},{2,0},{3,1},{4,6},{5,7},{6,4},{7,5},{8,10},{9,11},{10,... | collective-permute-start | bytes 1572872 | tf_op jit(solution)/shard_map/ppermute | solution.py:168
  198.8 24.0 %collective-permute-start.11 = (bf16[128,2048]{1,0:T(8,128)(2,1)S(1)}, bf16[128,2048]{1,0:T(8,128)(2,1)S(1)}, u32[]{:S(2)}, u32[]{:S(2)}) collective-permute-start(bf16[128,2048]{1,0:T(8,128)(2,1)S(1)} %get-tuple-element.56), channel_id=1, source_target_pairs={{0,2},{1,3},{2,0},{3,1},{4,6},{5,7},{6,4},{7,5},{8,10},{9,11},{10,... | collective-permute-start | bytes 1572872 | tf_op jit(solution)/shard_map/ppermute | solution.py:168
  199.3 11.4 %collective-permute-start.8 = (bf16[128,2048]{1,0:T(8,128)(2,1)S(1)}, bf16[128,2048]{1,0:T(8,128)(2,1)S(1)}, u32[]{:S(2)}, u32[]{:S(2)}) collective-permute-start(bf16[128,2048]{1,0:T(8,128)(2,1)S(1)} %get-tuple-element.56), channel_id=1, source_target_pairs={{0,1},{1,0},{2,3},{3,2},{4,5},{5,4},{6,7},{7,6},{8,9},{9,8},{10,11... | collective-permute-start | bytes 1572872 | tf_op jit(solution)/shard_map/ppermute | solution.py:164
  210.9 51.4 %collective-permute-start.10 = (bf16[1,128,2048]{2,1,0:T(8,128)(2,1)S(1)}, bf16[1,128,2048]{2,1,0:T(8,128)(2,1)S(1)}, u32[]{:S(2)}, u32[]{:S(2)}) collective-permute-start(bf16[1,128,2048]{2,1,0:T(8,128)(2,1)S(1)} %slice_bitcast_fusion.7), channel_id=1, source_target_pairs={{0,1},{1,0},{2,3},{3,2},{4,5},{5,4},{6,7},{7,6},{8,9},{9,8},{10,11... | collective-permute-start | bytes 1572872 | tf_op jit(solution)/shard_map/ppermute | solution.py:164
  222.8 23.3 %collective-permute-start.12 = (bf16[128,2048]{1,0:T(8,128)(2,1)S(1)}, bf16[128,2048]{1,0:T(8,128)(2,1)S(1)}, u32[]{:S(2)}, u32[]{:S(2)}) collective-permute-start(bf16[128,2048]{1,0:T(8,128)(2,1)S(1)} %collective-permute-done.11), channel_id=1, source_target_pairs={{0,1},{1,0},{2,3},{3,2},{4,5},{5,4},{6,7},{7,6},{8,9},{9,8},{10,11... | collective-permute-start | bytes 1572872 | tf_op jit(solution)/shard_map/ppermute | solution.py:164
  222.8 11.8 %collective-permute-start.14 = (bf16[128,2048]{1,0:T(8,128)(2,1)S(1)}, bf16[128,2048]{1,0:T(8,128)(2,1)S(1)}, u32[]{:S(2)}, u32[]{:S(2)}) collective-permute-start(bf16[128,2048]{1,0:T(8,128)(2,1)S(1)} %collective-permute-done.13), channel_id=1, source_target_pairs={{0,1},{1,0},{2,3},{3,2},{4,5},{5,4},{6,7},{7,6},{8,9},{9,8},{10,11... | collective-permute-start | bytes 1572872 | tf_op jit(solution)/shard_map/ppermute | solution.py:164
  234.5 25.5 %copy-start.2 = (bf16[256,2048]{1,0:T(8,128)(2,1)}, bf16[256,2048]{1,0:T(8,128)(2,1)S(1)}, u32[]{:S(2)}) copy-start(bf16[256,2048]{1,0:T(8,128)(2,1)S(1)} %shard_map.220) | copy-start | bytes 3145732
  246.2 12.1 %collective-permute-start.15 = (bf16[1,128,2048]{2,1,0:T(8,128)(2,1)S(1)}, bf16[1,128,2048]{2,1,0:T(8,128)(2,1)S(1)}, u32[]{:S(2)}, u32[]{:S(2)}) collective-permute-start(bf16[1,128,2048]{2,1,0:T(8,128)(2,1)S(1)} %slice_bitcast_fusion.5), channel_id=1, source_target_pairs={{0,1},{1,0},{2,3},{3,2},{4,5},{5,4},{6,7},{7,6},{8,9},{9,8},{10,11... | collective-permute-start | bytes 1572872 | tf_op jit(solution)/shard_map/ppermute | solution.py:164
  257.7 3.1 %collective-permute-start.18 = (bf16[1,128,2048]{2,1,0:T(8,128)(2,1)S(1)}, bf16[1,128,2048]{2,1,0:T(8,128)(2,1)S(1)}, u32[]{:S(2)}, u32[]{:S(2)}) collective-permute-start(bf16[1,128,2048]{2,1,0:T(8,128)(2,1)S(1)} %slice_bitcast_fusion.1), channel_id=1, source_target_pairs={{0,1},{1,0},{2,3},{3,2},{4,5},{5,4},{6,7},{7,6},{8,9},{9,8},{10,11... | collective-permute-start | bytes 1572872 | tf_op jit(solution)/shard_map/ppermute | solution.py:164
  258.4 14.8 %collective-permute-start.16 = (bf16[128,2048]{1,0:T(8,128)(2,1)S(1)}, bf16[128,2048]{1,0:T(8,128)(2,1)S(1)}, u32[]{:S(2)}, u32[]{:S(2)}) collective-permute-start(bf16[128,2048]{1,0:T(8,128)(2,1)S(1)} %fusion.39), channel_id=1, source_target_pairs={{0,2},{1,3},{2,0},{3,1},{4,6},{5,7},{6,4},{7,5},{8,10},{9,11},{10,... | collective-permute-start | bytes 1572872 | tf_op jit(solution)/shard_map/ppermute | solution.py:168
  260.8 17.4 %collective-permute-start.17 = (bf16[1,128,2048]{2,1,0:T(8,128)(2,1)}, bf16[1,128,2048]{2,1,0:T(8,128)(2,1)}, u32[]{:S(2)}, u32[]{:S(2)}) collective-permute-start(bf16[1,128,2048]{2,1,0:T(8,128)(2,1)} %slice_bitcast_fusion.3), channel_id=1, source_target_pairs={{0,1},{1,0},{2,3},{3,2},{4,5},{5,4},{6,7},{7,6},{8,9},{9,8},{10,11... | collective-permute-start | bytes 1572872 | tf_op jit(solution)/shard_map/ppermute | solution.py:164
  261.8 21.9 %collective-permute-start.19 = (bf16[128,2048]{1,0:T(8,128)(2,1)}, bf16[128,2048]{1,0:T(8,128)(2,1)}, u32[]{:S(2)}, u32[]{:S(2)}) collective-permute-start(bf16[128,2048]{1,0:T(8,128)(2,1)} %fusion.40), channel_id=1, source_target_pairs={{0,2},{1,3},{2,0},{3,1},{4,6},{5,7},{6,4},{7,5},{8,10},{9,11},{10,... | collective-permute-start | bytes 1572872 | tf_op jit(solution)/shard_map/ppermute | solution.py:168
  (31 other events, 178.4 us)

commit v2 on v1

--- a/solution.py
+++ b/solution.py
@@ -178,13 +178,19 @@
 
 def join_cores(partial, tp_count):
     came = swap_cores(partial[:, 1].astype(jnp.bfloat16), tp_count)
-    return partial[:, 0].astype(jnp.float32) + came.astype(jnp.float32)
-
-
-def join_chips(joined, total, tp_count):
-    for step in range(1, joined.shape[0] + 1):
-        came = shift_chips(joined[step - 1].astype(jnp.bfloat16), tp_count, -step)
-        total = total + came.astype(jnp.float32)
+    joined = partial[:, 0].astype(jnp.float32) + came.astype(jnp.float32)
+    return joined, joined.astype(jnp.bfloat16)
+
+
+def send_chips(leaving, tp_count):
+    return [
+        shift_chips(leaving[step - 1], tp_count, -step) for step in range(1, leaving.shape[0] + 1)
+    ]
+
+
+def add_all(total, pieces):
+    for piece in pieces:
+        total = total + piece.astype(jnp.float32)
     return total
 
 
@@ -299,6 +305,8 @@
         picked[:, :, None],
         (dp_count, KVH, sharing // 2, 2, capacity, page_len, head_dim),
     ).reshape(devices, capacity, page_len, head_dim)
+    near = spread_rows(hidden_in, tp_count)
+    outgoing, *near = lax.optimization_barrier((outgoing, *near))
     arrived = lax.all_to_all(outgoing, ("dp", "tensor"), split_axis=0, concat_axis=0, tiled=True)
     own_used = lax.dynamic_index_in_dim(group_used, dp_at, 0, keepdims=False)
     own_table = lax.dynamic_index_in_dim(group_table, dp_at, 0, keepdims=False)
@@ -309,7 +317,7 @@
     ).reshape(-1)
     place = jnp.where(own_used, own_table // pool_dev * capacity + present_rank[own_table], 0)
     own_lengths = lax.dynamic_slice_in_dim(cached_len, dp_at * REQ_DEV, REQ_DEV, 0)
-    near = jnp.stack(spread_rows(hidden_in, tp_count))
+    near = jnp.stack(near)
     gathered = jnp.concatenate(
         [
             lax.dynamic_index_in_dim(
@@ -362,11 +370,12 @@
     ]
     core_flag = core_at.reshape(1).astype(jnp.int32)
     width = hidden_in.shape[1]
-    joined = []
+    kept_rows, arriving = [], []
     for half in range(HALVES):
         half_queries = queries[:, :, half].reshape(REQ_DEV, new_count // HALVES, -1)
         if half:
-            half_queries, joined[-1] = lax.optimization_barrier((half_queries, joined[-1]))
+            half_queries, sent = lax.optimization_barrier((half_queries, sent))
+            arriving.append(send_chips(sent, tp_count))
         attended = attend(
             place,
             own_lengths,
@@ -378,34 +387,52 @@
             mine,
             other,
         ).reshape(tp_count, half_rows, -1)
+        if half:
+            attended, *arriving[-1] = lax.optimization_barrier((attended, *arriving[-1]))
         attended = jnp.concatenate(
             [lax.dynamic_index_in_dim(attended, owner, 0, keepdims=False) for owner in owners]
         )
         partial = jnp.dot(attended, w_out, preferred_element_type=jnp.float32)
-        joined.append(join_cores(partial.reshape(chips, 2, half_rows, width), tp_count))
-    mixed_halves, entering = [], []
+        joined, sent = join_cores(partial.reshape(chips, 2, half_rows, width), tp_count)
+        kept_rows.append(joined[0])
+        sent = sent[1:]
+    arriving.append(send_chips(sent, tp_count))
+    mixed_halves, entering, near_down = [], [], []
     for half in range(HALVES):
         rows = slice(half * half_rows, (half + 1) * half_rows)
-        projected = join_chips(joined[half][1:], joined[half][0], tp_count)
+        if half:
+            near_down[-1], *arriving[half] = lax.optimization_barrier(
+                (near_down[-1], *arriving[half])
+            )
+        projected = add_all(kept_rows[half], arriving[half])
         mixed_rows = (beside[rows] + norm_rows(projected, post_attn_gain)) * HALF_ROOT
         mixed_halves.append(mixed_rows)
         ffn_in = norm_rows(mixed_rows, pre_ffn_gain).astype(jnp.bfloat16)
-        entering.append(spread_rows(ffn_in, tp_count))
-    near_down, far_down = [], []
-    last = None
-    for pick, kept in ((slice(0, 2), near_down), (slice(2, None), far_down)):
-        for half in range(HALVES):
-            block = jnp.concatenate(entering[half][pick])
-            if last is not None:
-                block, last[-1] = lax.optimization_barrier((block, last[-1]))
-            kept.append(feed_forward(block, w_gate, w_up, w_down))
-            last = kept
+        came = [shift_chips(ffn_in, tp_count, step) for step in range(1, chips)]
+        entering.append((ffn_in, came))
+        block = jnp.concatenate([ffn_in, swap_cores(ffn_in, tp_count)])
+        near_down.append(feed_forward(block, w_gate, w_up, w_down))
+    far_sent = []
+    tie = near_down[-1]
+    for half in range(HALVES):
+        came = entering[half][1]
+        tie, *came = lax.optimization_barrier((tie, *came))
+        if half == 0:
+            near_down[-1] = tie
+        entering[half] = [piece for one in came for piece in (one, swap_cores(one, tp_count))]
+    for half in range(HALVES):
+        block = jnp.concatenate(entering[half])
+        if half:
+            block, far_sent[-1] = lax.optimization_barrier((block, far_sent[-1]))
+        far_down = feed_forward(block, w_gate, w_up, w_down)
+        far_sent.append(
+            join_cores(far_down.reshape(chips - 1, 2, half_rows, width), tp_count)[1]
+        )
     results = []
     for half in range(HALVES):
         rows = slice(half * half_rows, (half + 1) * half_rows)
-        near_sum = join_cores(near_down[half].reshape(1, 2, half_rows, width), tp_count)[0]
-        far_sum = join_cores(far_down[half].reshape(chips - 1, 2, half_rows, width), tp_count)
-        down = join_chips(far_sum, near_sum, tp_count)
+        near_sum = join_cores(near_down[half].reshape(1, 2, half_rows, width), tp_count)[0][0]
+        down = add_all(near_sum, send_chips(far_sent[half], tp_count))
         settled = mixed_halves[half] + norm_rows(down, post_ffn_gain)
         settled_half = settled.astype(jnp.bfloat16)
         gated = jax.nn.gelu(

time: 299 us -> 289 us (0.967)
  waiting for transfers between devices: 112 us -> 105 us
    ppermute x7, waiting for transfers between devices: 111 us -> 45.8 us  [shift_chips(): lax.ppermute(values, 'tensor', [(t, (t + 2 * step) % tp_count) for t in r...]
    all_to_all x1, waiting for transfers between devices: 0.01 us -> 54.2 us  [per_device(): lax.all_to_all(outgoing, ('dp', 'tensor'), split_axis=0, concat_axis=0, t...]
    ppermute x13, waiting for transfers between devices: 1.39 us -> 5.15 us  [swap_cores(): return lax.ppermute(values, 'tensor', [(t, t ^ 1) for t in range(tp_count)])]
    reduce_sum x7 -> x8, other arithmetic: 5.47 us -> 6.49 us  [norm_rows(): jnp.mean(values * values, axis=-1, keepdims=True) + EPS]
  transfers between devices with their start and end apart: 21 -> 21, of which waited for: 8 -> 10; matrix products, arithmetic and copies ran while one was open for 21% -> 24% of each run, Pallas kernels for 15% -> 20%
where the time goes in v2:
time: 289 us; the launch traced here: 284 us
  waiting for transfers between devices  105 us (36%)
  Pallas kernels  68 us (24%)
  other arithmetic  41.6 us (14%)
  matrix products  29.1 us (10%)
  local copies, waits for them, and re-layouts  22.2 us (8%)
  starting transfers between devices  17 us (6%)
    all_to_all x1, waiting for transfers between devices, per_device(): lax.all_to_all(outgoing, ('dp', 'tensor'), split_axis=0, concat_axis=0, t...  54.2 us
    ppermute x7, waiting for transfers between devices, shift_chips(): lax.ppermute(values, 'tensor', [(t, (t + 2 * step) % tp_count) for t in r...  45.8 us
    pallas_call x4, Pallas kernels, feed_forward(): pl.pallas_call(ffn_kernel, out_shape=jax.ShapeDtypeStruct(block.shape, jn...  45.2 us
    pallas_call x2, Pallas kernels, attend(): pl.pallas_call(functools.partial(attend_kernel, slots), out_shape=jax.Sha...  22.8 us
    ppermute x7, starting transfers between devices, shift_chips(): lax.ppermute(values, 'tensor', [(t, (t + 2 * step) % tp_count) for t in r...  8.89 us
    dot_general x2, matrix products, per_device(): jnp.dot(gated, ple_proj, preferred_element_type=jnp.float32)  7.72 us
    convert_element_type x1, other arithmetic, per_device(): norm_rows(gathered.astype(jnp.float32), norm_in).astype(jnp.bfloat16)  7.18 us
    reduce_sum x8, other arithmetic, norm_rows(): jnp.mean(values * values, axis=-1, keepdims=True) + EPS  6.49 us
  transfers between devices with their start and end apart: 21, of which 10 were waited for; matrix products, arithmetic and copies ran while one was open for 24% of the time, Pallas kernels for 20%

profile of v2, /device:TPU:0, one launch (start us, length us, event | category | flops | bytes accessed | tf_op | source)
XLA Modules:
  0.0 284.2 jit_solution(8818386867239982399)
XLA Ops:
  0.0 2.9 %collective-permute-start.1 = (bf16[256,2048]{1,0:T(8,128)(2,1)}, bf16[256,2048]{1,0:T(8,128)(2,1)S(1)}, u32[]{:S(2)}, u32[]{:S(2)}) collective-permute-start(bf16[256,2048]{1,0:T(8,128)(2,1)} %param.23), channel_id=1, source_target_pairs={{0,2},{1,3},{2,0},{3,1},{4,6},{5,7},{6,4},{7,5},{8,10},{9,11},{10,... | collective-permute-start | bytes 3145736 | tf_op jit(solution)/shard_map/ppermute | solution.py:168
  4.0 22.3 %collective-permute-done.1 = bf16[256,2048]{1,0:T(8,128)(2,1)S(1)} collective-permute-done((bf16[256,2048]{1,0:T(8,128)(2,1)}, bf16[256,2048]{1,0:T(8,128)(2,1)S(1)}, u32[]{:S(2)}, u32[]{:S(2)}) %collective-permute-start.1) | collective-permute-done | bytes 1048608 | tf_op jit(solution)/shard_map/ppermute | solution.py:168
  27.6 4.7 %convert_bitcast_fusion = bf16[8,2,2,2,128,256]{5,0,4,1,2,3:T(8,128)(2,1)S(1)} fusion(bf16[16,2,2,128,256]{4,3,2,1,0:T(8,128)(2,1)} %param.27, s32[8,16]{1,0:T(8,128)S(1)} %broadcast_add_fusion.1, pred[8,16]{1,0:T(8,128)(4,1)S(1)} %and_reduce_fusion), kind=kOutput, calls=%fused_computation.11 | convolution fusion | flops 69206528 | bytes 8389248 | tf_op jit(solution)/shard_map/dcl,lkhpe->dhkcpe/dot_general | solution.py:301
  32.3 3.0 %copy.48 = bf16[8,2,2,2,128,256]{5,4,3,2,1,0:T(8,128)(2,1)} copy(bf16[8,2,2,2,128,256]{5,0,4,1,2,3:T(8,128)(2,1)S(1)} %convert_bitcast_fusion) | data formatting | bytes 8388608 | tf_op jit(solution)/shard_map/convert_element_type | solution.py:303
  35.3 6.5 %all-to-all-start = ((bf16[32,2,128,256]{3,2,1,0:T(8,128)(2,1)}), bf16[32,2,128,256]{3,2,1,0:T(8,128)(2,1)}, u32[]{:S(2)}, u32[]{:S(2)}) async-start(bf16[32,2,128,256]{3,2,1,0:T(8,128)(2,1)} %bitcast.228), calls=%async_computation | async-start | bytes 8388608 | tf_op jit(solution)/shard_map/all_to_all | solution.py:310
  42.1 3.1 %multiply_cosine_fusion.1 = (f32[1024,128]{1,0:T(8,128)}, f32[1024,128]{1,0:T(8,128)}) fusion(f32[128]{0:T(128)S(1)} %multiply_exponential_fusion, f32[1024]{0:T(1024)S(1)} %bitcast.237), kind=kLoop, calls=%fused_computation.87 | loop fusion | flops 131072 | bytes 1053184 | tf_op jit(solution)/shard_map/cos | solution.py:32
  48.9 7.2 %fusion.2 = bf16[1024,2048]{1,0:T(8,128)(2,1)S(1)} fusion(f32[2048]{0:T(1024)S(1)} %copy-done.25, f32[1024]{0:T(1024)S(1)} %add_rsqrt_fusion.3, bf16[256,2048]{1,0:T(8,128)(2,1)S(1)} %get-tuple-element.50, bf16[256,2048]{1,0:T(8,128)(2,1)S(1)} %get-tuple-element.51, bf16[256,2048]{1,0:T(8,128)(2,1)S(1)} %get-tuple-element.52, ...), kind=kLoop, calls=%fused_computation.5 | loop fusion | flops 23068672 | bytes 8400896 | tf_op jit(solution)/shard_map/convert_element_type | solution.py:331
  56.1 3.7 %multiply_reduce_fusion = (f32[1024,2]{0,1:T(2,128)S(1)}, f32[1024,512]{0,1:T(8,128)}) fusion(bf16[1024,2048]{1,0:T(8,128)(2,1)S(1)} %fusion.2, bf16[2048,512]{1,0:T(8,128)(2,1)S(1)} %copy-done.33), kind=kOutput, calls=%fused_computation.25 | convolution fusion | flops 2148530176 | bytes 8396800 | tf_op jit(solution)/shard_map/dot_general | solution.py:334
  59.8 4.1 %copy.50 = f32[1024,2,256]{2,1,0:T(2,128)} copy(f32[1024,2,256]{0,2,1:T(8,128)} %bitcast.234) | data formatting | bytes 4194304 | tf_op jit(solution)/shard_map/reshape | solution.py:334
  64.2 3.8 %multiply_reduce_fusion.11 = (f32[1024]{0:T(1024)S(1)}, f32[1024,256]{0,1:T(8,128)S(1)}) fusion(bf16[1024,2048]{1,0:T(8,128)(2,1)} %copy-done.18, bf16[2048,1024]{1,0:T(8,128)(2,1)} %param.30, s32[]{:T(128)S(6)} %select_n.135), kind=kOutput, calls=%fused_computation.74 | convolution fusion | flops 1074265088 | bytes 6295556 | tf_op jit(solution)/shard_map/dot_general | solution.py:340
  72.6 2.6 multiply_multiply_fusion
  81.6 54.2 %all-to-all-done = bf16[32,2,128,256]{3,2,1,0:T(8,128)(2,1)} async-done(((bf16[32,2,128,256]{3,2,1,0:T(8,128)(2,1)}), bf16[32,2,128,256]{3,2,1,0:T(8,128)(2,1)}, u32[]{:S(2)}, u32[]{:S(2)}) %all-to-all-start) | async-done | bytes 4194336 | tf_op jit(solution)/shard_map/all_to_all | solution.py:310
  143.2 11.1 %shard_map.217 = bf16[2,256,512]{2,1,0:T(8,128)(2,1)S(1)} custom-call(s32[64]{0:T(128)S(1)} %add_select_fusion.place, s32[2]{0:T(128)S(1)} %dynamic_slice.57.lengths, s32[1]{0:T(128)} %bitcast.4.core, bf16[2,256,512]{2,1,0:T(8,128)(2,1)S(1)} %bitcast.227, s32[256,1]{1,0:T(8,128)S(1)} %copy.52.off_ref, bf16[2,512,256]{2,1,0:T(8,128)(2,1)S(1)} %bitcast.222, ...), custom_call_target="tpu_custom_call" | custom-call | flops 4831838208 | bytes 8388608 | tf_op jit(solution)/shard_map/pallas_call | solution.py:134
  158.0 4.1 %multiply_reduce_fusion.1 = (f32[256]{0:T(256)S(1)}, f32[256,2048]{1,0:T(8,128)}) fusion(bf16[64,2048]{1,0:T(8,128)(2,1)S(1)} %copy-done.23, bf16[2048,64]{0,1:T(8,128)(2,1)} %param.35, bf16[256,2048]{1,0:T(8,128)(2,1)} %param.23, f32[2048]{0:T(1024)S(1)} %copy-done.25, f32[256]{0:T(256)S(1)} %add_rsqrt_fusion.5), kind=kOutput, calls=%fused_computation.26 | convolution fusion | flops 137379584 | bytes 3680256 | tf_op jit(solution)/shard_map/dot_general | solution.py:362
  169.8 11.7 %shard_map.218 = bf16[2,256,512]{2,1,0:T(8,128)(2,1)S(1)} custom-call(s32[64]{0:T(128)S(1)} %add_select_fusion.place, s32[2]{0:T(128)S(1)} %dynamic_slice.57.lengths, s32[1]{0:T(128)} %bitcast.4.core, bf16[2,256,512]{2,1,0:T(8,128)(2,1)S(1)} %bitcast.226, s32[256,1]{1,0:T(8,128)S(1)} %copy.55.off_ref, bf16[2,512,256]{2,1,0:T(8,128)(2,1)S(1)} %bitcast.223, ...), custom_call_target="tpu_custom_call" | custom-call | flops 4831838208 | bytes 8388608 | tf_op jit(solution)/shard_map/pallas_call | solution.py:134
  190.7 11.3 %shard_map.219 = bf16[256,2048]{1,0:T(8,128)(2,1)S(1)} custom-call(bf16[256,2048]{1,0:T(8,128)(2,1)S(1)} %pad_maximum_fusion.3.x_ref, bf16[2048,2048]{1,0:T(8,128)(2,1)S(1)} %bitcast.207, bf16[2048,2048]{1,0:T(8,128)(2,1)} %up_ref.7, bf16[2048,2048]{1,0:T(8,128)(2,1)} %down_ref.7), custom_call_target="tpu_custom_call" | custom-call | flops 6442450944 | bytes 25165824 | tf_op jit(solution)/shard_map/pallas_call | solution.py:222
  206.9 11.3 %shard_map.220 = bf16[256,2048]{1,0:T(8,128)(2,1)S(1)} custom-call(bf16[256,2048]{1,0:T(8,128)(2,1)S(1)} %pad_maximum_fusion.4.x_ref, bf16[2048,2048]{1,0:T(8,128)(2,1)S(1)} %bitcast.207, bf16[2048,2048]{1,0:T(8,128)(2,1)} %up_ref.7, bf16[2048,2048]{1,0:T(8,128)(2,1)} %down_ref.7), custom_call_target="tpu_custom_call" | custom-call | flops 6442450944 | bytes 25165824 | tf_op jit(solution)/shard_map/pallas_call | solution.py:222
  219.5 10.8 %collective-permute-done.12 = bf16[128,2048]{1,0:T(8,128)(2,1)S(1)} collective-permute-done((bf16[128,2048]{1,0:T(8,128)(2,1)S(1)}, bf16[128,2048]{1,0:T(8,128)(2,1)S(1)}, u32[]{:S(2)}, u32[]{:S(2)}) %collective-permute-start.12) | collective-permute-done | bytes 524320 | tf_op jit(solution)/shard_map/ppermute | solution.py:168
  230.4 11.3 %shard_map.221 = bf16[256,2048]{1,0:T(8,128)(2,1)S(1)} custom-call(bf16[256,2048]{1,0:T(8,128)(2,1)S(1)} %pad_maximum_fusion.6.x_ref, bf16[2048,2048]{1,0:T(8,128)(2,1)S(1)} %bitcast.207, bf16[2048,2048]{1,0:T(8,128)(2,1)} %up_ref.7, bf16[2048,2048]{1,0:T(8,128)(2,1)} %down_ref.7), custom_call_target="tpu_custom_call" | custom-call | flops 6442450944 | bytes 25165824 | tf_op jit(solution)/shard_map/pallas_call | solution.py:222
  244.9 11.4 %shard_map.222 = bf16[256,2048]{1,0:T(8,128)(2,1)S(1)} custom-call(bf16[256,2048]{1,0:T(8,128)(2,1)S(1)} %pad_maximum_fusion.5.x_ref, bf16[2048,2048]{1,0:T(8,128)(2,1)S(1)} %bitcast.207, bf16[2048,2048]{1,0:T(8,128)(2,1)} %up_ref.7, bf16[2048,2048]{1,0:T(8,128)(2,1)} %down_ref.7), custom_call_target="tpu_custom_call" | custom-call | flops 6442450944 | bytes 25165824 | tf_op jit(solution)/shard_map/pallas_call | solution.py:222
  260.5 4.0 %multiply_reduce_fusion.4 = (f32[128]{0:T(128)S(1)}, f32[128,2048]{1,0:T(8,128)}) fusion(bf16[256,2048]{1,0:T(8,128)(2,1)} %param.44, bf16[2048,256]{1,0:T(8,128)(2,1)} %param.43, bf16[256,256]{1,0:T(8,128)(2,1)S(1)} %copy-done.24, f32[128,2048]{1,0:T(8,128)} %copy-done.5, bf16[128,2048]{1,0:T(8,128)(2,1)} %copy-done.17, ...), kind=kOutput, calls=%fused_computation.60 | convolution fusion | flops 271941504 | bytes 5841920 | tf_op jit(solution)/shard_map/dot_general | solution.py:446
  264.5 9.0 %collective-permute-done.19 = bf16[128,2048]{1,0:T(8,128)(2,1)} collective-permute-done((bf16[128,2048]{1,0:T(8,128)(2,1)}, bf16[128,2048]{1,0:T(8,128)(2,1)}, u32[]{:S(2)}, u32[]{:S(2)}) %collective-permute-start.19) | collective-permute-done | bytes 524320 | tf_op jit(solution)/shard_map/ppermute | solution.py:168
  275.1 3.7 %multiply_reduce_fusion.2 = (f32[128]{0:T(128)S(1)}, f32[128,2048]{1,0:T(8,128)}) fusion(bf16[256,2048]{1,0:T(8,128)(2,1)} %param.44, bf16[2048,256]{1,0:T(8,128)(2,1)} %param.43, bf16[256,256]{1,0:T(8,128)(2,1)S(1)} %copy-done.24, f32[128,2048]{1,0:T(8,128)S(1)} %copy-done.7, bf16[128,2048]{1,0:T(8,128)(2,1)} %collective-permute-done.19, ...), kind=kOutput, calls=%fused_computation.56 | convolution fusion | flops 271941504 | bytes 5841920 | tf_op jit(solution)/shard_map/dot_general | solution.py:446
  278.8 4.1 %add_convert_fusion.1 = (bf16[128,2048]{1,0:T(8,128)(2,1)S(1)}, bf16[128,2048]{1,0:T(8,128)(2,1)S(1)}) fusion(f32[128,2048]{1,0:T(8,128)} %get-tuple-element.84, f32[2048]{0:T(1024)S(1)} %copy-done.30, f32[128]{0:T(128)S(1)} %add_rsqrt_fusion.8, f32[2048]{0:T(1024)S(1)} %copy-done.26, f32[128]{0:T(128)S(1)} %add_rsqrt_fusion.9, ...), kind=kLoop, calls=%fused_computation.59 | loop fusion | flops 6815744 | bytes 8407040 | tf_op jit(solution)/shard_map/convert_element_type | solution.py:448
  (205 shorter events, 61.4 us)
Async XLA Ops:
  0.0 154.4 %copy-start = (bf16[512,2048]{1,0:T(8,128)(2,1)S(1)}, bf16[512,2048]{1,0:T(8,128)(2,1)}, u32[]{:S(2)}) copy-start(bf16[512,2048]{1,0:T(8,128)(2,1)} %param.33) | copy-start | bytes 6291460
  0.0 26.3 %collective-permute-start.1 = (bf16[256,2048]{1,0:T(8,128)(2,1)}, bf16[256,2048]{1,0:T(8,128)(2,1)S(1)}, u32[]{:S(2)}, u32[]{:S(2)}) collective-permute-start(bf16[256,2048]{1,0:T(8,128)(2,1)} %param.23), channel_id=1, source_target_pairs={{0,2},{1,3},{2,0},{3,1},{4,6},{5,7},{6,4},{7,5},{8,10},{9,11},{10,... | collective-permute-start | bytes 3145736 | tf_op jit(solution)/shard_map/ppermute | solution.py:168
  2.9 32.3 %collective-permute-start = (bf16[256,2048]{1,0:T(8,128)(2,1)}, bf16[256,2048]{1,0:T(8,128)(2,1)}, u32[]{:S(2)}, u32[]{:S(2)}) collective-permute-start(bf16[256,2048]{1,0:T(8,128)(2,1)} %param.23), channel_id=1, source_target_pairs={{0,1},{1,0},{2,3},{3,2},{4,5},{5,4},{6,7},{7,6},{8,9},{9,8},{10,11... | collective-permute-start | bytes 3145736 | tf_op jit(solution)/shard_map/ppermute | solution.py:164
  26.3 9.0 %collective-permute-start.2 = (bf16[256,2048]{1,0:T(8,128)(2,1)S(1)}, bf16[256,2048]{1,0:T(8,128)(2,1)}, u32[]{:S(2)}, u32[]{:S(2)}) collective-permute-start(bf16[256,2048]{1,0:T(8,128)(2,1)S(1)} %collective-permute-done.1), channel_id=1, source_target_pairs={{0,1},{1,0},{2,3},{3,2},{4,5},{5,4},{6,7},{7,6},{8,9},{9,8},{10,11... | collective-permute-start | bytes 3145736 | tf_op jit(solution)/shard_map/ppermute | solution.py:164
  35.3 100.4 %all-to-all-start = ((bf16[32,2,128,256]{3,2,1,0:T(8,128)(2,1)}), bf16[32,2,128,256]{3,2,1,0:T(8,128)(2,1)}, u32[]{:S(2)}, u32[]{:S(2)}) async-start(bf16[32,2,128,256]{3,2,1,0:T(8,128)(2,1)} %bitcast.228), calls=%async_computation | async-start | bytes 8388608 | tf_op jit(solution)/shard_map/all_to_all | solution.py:310
  135.7 7.5 %collective-permute-start.3 = (bf16[64,128,256]{2,1,0:T(8,128)(2,1)}, bf16[64,128,256]{2,1,0:T(8,128)(2,1)}, u32[]{:S(2)}, u32[]{:S(2)}) collective-permute-start(bf16[64,128,256]{2,1,0:T(8,128)(2,1)} %bitcast.24.mine), channel_id=1, source_target_pairs={{0,1},{1,0},{2,3},{3,2},{4,5},{5,4},{6,7},{7,6},{8,9},{9,8},{10,11... | collective-permute-start | bytes 12582920 | tf_op jit(solution)/shard_map/ppermute | solution.py:164
  156.8 5.3 %collective-permute-start.4 = (bf16[2,128,2048]{2,1,0:T(8,128)(2,1)}, bf16[2,128,2048]{2,1,0:T(8,128)(2,1)}, u32[]{:S(2)}, u32[]{:S(2)}) collective-permute-start(bf16[2,128,2048]{2,1,0:T(8,128)(2,1)} %fusion.14), channel_id=1, source_target_pairs={{0,1},{1,0},{2,3},{3,2},{4,5},{5,4},{6,7},{7,6},{8,9},{9,8},{10,11... | collective-permute-start | bytes 3145736 | tf_op jit(solution)/shard_map/ppermute | solution.py:164
  165.4 16.1 %collective-permute-start.5 = (bf16[128,2048]{1,0:T(8,128)(2,1)}, bf16[128,2048]{1,0:T(8,128)(2,1)}, u32[]{:S(2)}, u32[]{:S(2)}) collective-permute-start(bf16[128,2048]{1,0:T(8,128)(2,1)} %bitcast.37), channel_id=1, source_target_pairs={{0,2},{1,3},{2,0},{3,1},{4,6},{5,7},{6,4},{7,5},{8,10},{9,11},{10,... | collective-permute-start | bytes 1572872 | tf_op jit(solution)/shard_map/ppermute | solution.py:168
  185.8 3.6 %collective-permute-start.7 = (bf16[2,128,2048]{2,1,0:T(8,128)(2,1)S(1)}, bf16[2,128,2048]{2,1,0:T(8,128)(2,1)S(1)}, u32[]{:S(2)}, u32[]{:S(2)}) collective-permute-start(bf16[2,128,2048]{2,1,0:T(8,128)(2,1)S(1)} %fusion.15), channel_id=1, source_target_pairs={{0,1},{1,0},{2,3},{3,2},{4,5},{5,4},{6,7},{7,6},{8,9},{9,8},{10,11... | collective-permute-start | bytes 3145736 | tf_op jit(solution)/shard_map/ppermute | solution.py:164
  186.8 2.5 collective-permute-start.6
  189.8 14.0 %collective-permute-start.8 = (bf16[128,2048]{1,0:T(8,128)(2,1)S(1)}, bf16[128,2048]{1,0:T(8,128)(2,1)S(1)}, u32[]{:S(2)}, u32[]{:S(2)}) collective-permute-start(bf16[128,2048]{1,0:T(8,128)(2,1)S(1)} %fusion.41), channel_id=1, source_target_pairs={{0,2},{1,3},{2,0},{3,1},{4,6},{5,7},{6,4},{7,5},{8,10},{9,11},{10,... | collective-permute-start | bytes 1572872 | tf_op jit(solution)/shard_map/ppermute | solution.py:168
  204.7 2.2 collective-permute-start.10
  204.7 14.8 %collective-permute-start.11 = (bf16[128,2048]{1,0:T(8,128)(2,1)S(1)}, bf16[128,2048]{1,0:T(8,128)(2,1)S(1)}, u32[]{:S(2)}, u32[]{:S(2)}) collective-permute-start(bf16[128,2048]{1,0:T(8,128)(2,1)S(1)} %multiply_convert_fusion.1), channel_id=1, source_target_pairs={{0,2},{1,3},{2,0},{3,1},{4,6},{5,7},{6,4},{7,5},{8,10},{9,11},{10,... | collective-permute-start | bytes 1572872 | tf_op jit(solution)/shard_map/ppermute | solution.py:168
  205.6 24.7 %collective-permute-start.12 = (bf16[128,2048]{1,0:T(8,128)(2,1)S(1)}, bf16[128,2048]{1,0:T(8,128)(2,1)S(1)}, u32[]{:S(2)}, u32[]{:S(2)}) collective-permute-start(bf16[128,2048]{1,0:T(8,128)(2,1)S(1)} %multiply_convert_fusion), channel_id=1, source_target_pairs={{0,2},{1,3},{2,0},{3,1},{4,6},{5,7},{6,4},{7,5},{8,10},{9,11},{10,... | collective-permute-start | bytes 1572872 | tf_op jit(solution)/shard_map/ppermute | solution.py:168
  218.2 38.3 %copy-start.2 = (bf16[256,2048]{1,0:T(8,128)(2,1)}, bf16[256,2048]{1,0:T(8,128)(2,1)S(1)}, u32[]{:S(2)}) copy-start(bf16[256,2048]{1,0:T(8,128)(2,1)S(1)} %shard_map.220) | copy-start | bytes 3145732
  219.5 10.8 %collective-permute-start.14 = (bf16[128,2048]{1,0:T(8,128)(2,1)S(1)}, bf16[128,2048]{1,0:T(8,128)(2,1)S(1)}, u32[]{:S(2)}, u32[]{:S(2)}) collective-permute-start(bf16[128,2048]{1,0:T(8,128)(2,1)S(1)} %collective-permute-done.11), channel_id=1, source_target_pairs={{0,1},{1,0},{2,3},{3,2},{4,5},{5,4},{6,7},{7,6},{8,9},{9,8},{10,11... | collective-permute-start | bytes 1572872 | tf_op jit(solution)/shard_map/ppermute | solution.py:164
  230.3 12.1 %collective-permute-start.13 = (bf16[128,2048]{1,0:T(8,128)(2,1)S(1)}, bf16[128,2048]{1,0:T(8,128)(2,1)S(1)}, u32[]{:S(2)}, u32[]{:S(2)}) collective-permute-start(bf16[128,2048]{1,0:T(8,128)(2,1)S(1)} %collective-permute-done.12), channel_id=1, source_target_pairs={{0,1},{1,0},{2,3},{3,2},{4,5},{5,4},{6,7},{7,6},{8,9},{9,8},{10,11... | collective-permute-start | bytes 1572872 | tf_op jit(solution)/shard_map/ppermute | solution.py:164
  241.7 2.1 collective-permute-start.15
  242.4 15.4 %collective-permute-start.9 = (bf16[1,128,2048]{2,1,0:T(8,128)(2,1)S(1)}, bf16[1,128,2048]{2,1,0:T(8,128)(2,1)S(1)}, u32[]{:S(2)}, u32[]{:S(2)}) collective-permute-start(bf16[1,128,2048]{2,1,0:T(8,128)(2,1)S(1)} %slice_bitcast_fusion.8), channel_id=1, source_target_pairs={{0,1},{1,0},{2,3},{3,2},{4,5},{5,4},{6,7},{7,6},{8,9},{9,8},{10,11... | collective-permute-start | bytes 1572872 | tf_op jit(solution)/shard_map/ppermute | solution.py:164
  244.0 14.3 %collective-permute-start.16 = (bf16[128,2048]{1,0:T(8,128)(2,1)S(1)}, bf16[128,2048]{1,0:T(8,128)(2,1)S(1)}, u32[]{:S(2)}, u32[]{:S(2)}) collective-permute-start(bf16[128,2048]{1,0:T(8,128)(2,1)S(1)} %bitcast.236), channel_id=1, source_target_pairs={{0,2},{1,3},{2,0},{3,1},{4,6},{5,7},{6,4},{7,5},{8,10},{9,11},{10,... | collective-permute-start | bytes 1572872 | tf_op jit(solution)/shard_map/ppermute | solution.py:168
  256.3 2.3 collective-permute-start.18
  257.3 7.2 %collective-permute-start.17 = (bf16[1,128,2048]{2,1,0:T(8,128)(2,1)}, bf16[1,128,2048]{2,1,0:T(8,128)(2,1)}, u32[]{:S(2)}, u32[]{:S(2)}) collective-permute-start(bf16[1,128,2048]{2,1,0:T(8,128)(2,1)} %slice_bitcast_fusion.4), channel_id=1, source_target_pairs={{0,1},{1,0},{2,3},{3,2},{4,5},{5,4},{6,7},{7,6},{8,9},{9,8},{10,11... | collective-permute-start | bytes 1572872 | tf_op jit(solution)/shard_map/ppermute | solution.py:164
  259.5 14.0 %copy-start.3 = (bf16[256,2048]{1,0:T(8,128)(2,1)S(1)}, bf16[256,2048]{1,0:T(8,128)(2,1)}, u32[]{:S(2)}) copy-start(bf16[256,2048]{1,0:T(8,128)(2,1)} %copy-done.2) | copy-start | bytes 3145732
  259.6 14.0 %collective-permute-start.19 = (bf16[128,2048]{1,0:T(8,128)(2,1)}, bf16[128,2048]{1,0:T(8,128)(2,1)}, u32[]{:S(2)}, u32[]{:S(2)}) collective-permute-start(bf16[128,2048]{1,0:T(8,128)(2,1)} %fusion.40), channel_id=1, source_target_pairs={{0,2},{1,3},{2,0},{3,1},{4,6},{5,7},{6,4},{7,5},{8,10},{9,11},{10,... | collective-permute-start | bytes 1572872 | tf_op jit(solution)/shard_map/ppermute | solution.py:168
  (34 other events, 160.6 us)
